TPU v7x, 32 devices: a whole 2x2x4 slice. The times are simulated.
32 devices in a mesh: wide: 8 (over z, x), narrow: 4 (over y, core).
Axes of the slice: x: 2, y: 2, z: 4, core: 2. Of those that a mesh axis runs over, the one named last changes fastest.
Arguments:
- tokens: bfloat16 [32768, 768], P(('narrow', 'wide')), may hold values from -15 to 15
- cotangent: bfloat16 [32768, 768], P(('narrow', 'wide')), may hold values from -15 to 15
- lengths: int32 [32, 24], P(('narrow', 'wide')), may hold values from 1 to 202, 1024 in all within a row
- projection: float32 [64, 32], replicated, may hold values from -4 to 4
- inward: float32 [3, 768, 768], P(None, 'wide'), may hold values from -0.21875 to 0.21875
- outward: float32 [768, 768], P('wide'), may hold values from -0.875 to 0.875
- expand: float32 [768, 3072], P('wide'), may hold values from -0.21875 to 0.21875
- shrink: float32 [3072, 768], P('wide'), may hold values from -0.109375 to 0.109375
- vectors: float32 [13, 768], replicated, may hold values from -1.2 to 2
- inward_rows: float32 [3, 768], P(None, 'wide'), may hold values from 2293.76 to 62259.2
- inward_columns: float32 [3, 768], replicated, may hold values from 12451.84 to 49152
- outward_rows: float32 [768], P('wide'), may hold values from 294.912 to 7536.64
- outward_columns: float32 [768], replicated, may hold values from 1540.096 to 6225.92
- expand_rows: float32 [768], P('wide'), may hold values from 229.376 to 5898.24
- expand_columns: float32 [3072], replicated, may hold values from 1179.648 to 4587.52
- shrink_rows: float32 [3072], P('wide'), may hold values from 720.896 to 19005.44
- shrink_columns: float32 [768], replicated, may hold values from 3833.856 to 15400.96
- vector_state: float32 [13, 768], replicated, may hold values from 983.04 to 124518.4
Outputs:
- block_out: float32 [32768, 768], P(('narrow', 'wide'))
- input_grad: float32 [32768, 768], P(('narrow', 'wide'))
- inward_grad: float32 [3, 768, 768], P(None, 'wide')
- outward_grad: float32 [768, 768], P('wide')
- expand_grad: float32 [768, 3072], P('wide')
- shrink_grad: float32 [3072, 768], P('wide')
- vector_grad: float32 [13, 768], replicated
- inward_rows_next: float32 [3, 768], P(None, 'wide')
- inward_columns_next: float32 [3, 768], replicated
- outward_rows_next: float32 [768], P('wide')
- outward_columns_next: float32 [768], replicated
- expand_rows_next: float32 [768], P('wide')
- expand_columns_next: float32 [3072], replicated
- shrink_rows_next: float32 [3072], P('wide')
- shrink_columns_next: float32 [768], replicated
- vector_state_next: float32 [13, 768], replicated
- inward_next: float32 [3, 768, 768], P(None, 'wide')
- outward_next: float32 [768, 768], P('wide')
- expand_next: float32 [768, 3072], P('wide')
- shrink_next: float32 [3072, 768], P('wide')
- vectors_next: float32 [13, 768], replicated
Inputs may be any that keep to these rules, and one draw needn't show every extreme that they name: `lengths`: each row holds the token counts of the molecules of one sequence in order; a row sums to 1024 and its largest entry is 202.
All inputs are finite; a program needn't handle non-finite values.
Results may differ from a plain program's by a relative error of at most 0.008.
The roundings to bfloat16 on the way count: a program that leaves them out, or rounds other values in their place, can miss the bound.
Values may be sent and summed in bfloat16 or wider, within the bound.
No kernel may reach another device: no remote copies, remote signals or barrier semaphores. Data moves between devices by JAX's collectives and lax.ppermute only.
A program may use at most 112 MiB of HBM per device.

v0:
```python
import functools
import math

import jax
import jax.numpy as jnp
import numpy as np
from jax import lax
from jax.experimental import pallas as pl
from jax.experimental.pallas import tpu as pltpu
from jax.sharding import PartitionSpec as P

D = 768
HEADS = 12
HD = 64
FF = 3072
FEAT = 32
STEP = 10
LEN = 1024
SPAN = 256
CHUNKS = 3
GROUPS = 3
WIDTH = 256
FFC = FF // CHUNKS

norm_eps = 1e-05
square_eps = 1e-30
clip_level = 1.0

F32 = jnp.float32
BF16 = jnp.bfloat16
VMEM_LIMIT = 60 * 1024 * 1024
REST_LIMIT = 54 * 1024 * 1024
BACK_LIMIT = 46 * 1024 * 1024


def mm(left, right):
    return lax.dot_general(left, right, (((1,), (0,)), ((), ())), preferred_element_type=F32)


def mm_nt(left, right):
    return lax.dot_general(left, right, (((1,), (1,)), ((), ())), preferred_element_type=F32)


def mm_tn(left, right):
    return lax.dot_general(left, right, (((0,), (0,)), ((), ())), preferred_element_type=F32)


def halves(values):
    high = values.astype(BF16)
    return high, (values - high.astype(F32)).astype(BF16)


TAIL = (
    0.1795078068971634,
    0.17978088557720184,
    0.14234966039657593,
    0.06379217654466629,
    0.0434231162071228,
    -0.261725515127182,
    0.20454804599285126,
    -0.05167665705084801,
)


def normal_parts(values):
    size = jnp.abs(values)
    t = 1.0 / (1.0 + 0.45 * size)
    poly = TAIL[-1]
    for coeff in TAIL[-2::-1]:
        poly = poly * t + coeff
    bell = jnp.exp(-0.5 * values * values)
    tail = poly * t * bell
    return jnp.where(values >= 0, 1.0 - tail, tail), bell * 0.3989422804014327


def transposed(values):
    row = lax.broadcasted_iota(jnp.int32, (256, 256), 0)
    col = lax.broadcasted_iota(jnp.int32, (256, 256), 1)
    eye = (row == col).astype(F32).astype(BF16)
    return mm_nt(eye, values).astype(BF16)


def head_perm():
    perm = np.zeros((WIDTH, WIDTH), np.float32)
    for head in range(4):
        for half in range(2):
            for i in range(32):
                perm[head * 64 + half * 32 + i, half * 128 + head * 32 + i] = 1.0
    return perm


def make_blocks(lengths, base, first, last):
    def step(s, carry):
        count, begin, begin_row, end = carry
        new_end = end + lengths[0, s]
        full = new_end - begin_row > SPAN

        @pl.when(full)
        def _():
            base[count] = begin_row
            first[count] = begin
            last[count] = s - 1

        row = jnp.minimum((end // 16) * 16, LEN - SPAN)
        return (
            jnp.where(full, count + 1, count),
            jnp.where(full, s, begin),
            jnp.where(full, row, begin_row),
            new_end,
        )

    segments = lengths.shape[1]
    zero = jnp.int32(0)
    count, begin, begin_row, _ = lax.fori_loop(0, segments, step, (zero, zero, zero, zero))
    base[count] = begin_row
    first[count] = begin
    last[count] = segments - 1
    return count + 1


def lane_mask(lo, hi, width, dtype):
    lane = lax.broadcasted_iota(jnp.int32, (1, width), 1)
    return ((lane >= lo) & (lane < hi)).astype(F32).astype(dtype)


def value_rows(v_pair, head):
    keep = lane_mask(64 * head, 64 * head + 64, 128, BF16)
    return jnp.concatenate([v_pair * keep, jnp.broadcast_to(keep, v_pair.shape)], axis=1)


def span_mask(onehot, rows, lo, hi):
    member = onehot[rows, :]
    lane = lax.broadcasted_iota(jnp.int32, (1, 128), 1)
    inside = ((lane >= lo) & (lane <= hi)).astype(F32).astype(BF16)
    return mm_nt(member * inside, member).astype(BF16)


def cost(flops, size):
    return pl.CostEstimate(flops=10**6, transcendentals=0, bytes_accessed=10**5)


def row_blocks(body, loop=False):
    if not loop:
        for rows in range(0, LEN, 256):
            body(pl.ds(rows, 256))
        return

    def step(index, carry):
        body(pl.ds(pl.multiple_of(index * 256, 256), 256))
        return carry

    lax.fori_loop(0, LEN // 256, step, 0)


def any_spec():
    return pl.BlockSpec(memory_space=pl.ANY)


def in_copies(place, pieces, dst, sems, unit):
    if len(pieces) == 1:
        rows = dst.shape[1] // 3
        here = pl.ds(unit * rows, rows)
        return [pltpu.make_async_copy(pieces[0].at[:, here], dst.at[:, here], sems.at[unit, 0])]
    z, x, core = place[0], place[1], place[3]
    part, index = (0, unit) if unit < 2 else (4, 0)
    copies = []
    for side in range(2):
        half = core if side == 0 else 1 - core
        for flip in range(2):
            column = x if flip == 0 else 1 - x
            for shift in range(4):
                row = lax.rem(z + 4 - shift, 4) * 2 + column
                start = pl.multiple_of(unit * 96 + half * 48, 16)
                copies.append(
                    pltpu.make_async_copy(
                        pieces[part + 2 * side + flip].at[shift, index],
                        dst.at[row, pl.ds(start, 48)],
                        sems.at[unit, len(copies)],
                    )
                )
    return copies


def flat_copies(place, pieces, dst, sems):
    if len(pieces) == 1:
        return [pltpu.make_async_copy(pieces[0], dst, sems.at[0])]
    z, x, core = place[0], place[1], place[3]
    span = dst.shape[1] // 2
    copies = []
    for side in range(2):
        half = core if side == 0 else 1 - core
        for flip in range(2):
            column = x if flip == 0 else 1 - x
            for shift in range(4):
                row = lax.rem(z + 4 - shift, 4) * 2 + column
                start = pl.multiple_of(half * span, 16)
                copies.append(
                    pltpu.make_async_copy(
                        pieces[2 * side + flip].at[shift],
                        dst.at[row, pl.ds(start, span)],
                        sems.at[len(copies)],
                    )
                )
    return copies


def attend_kernel(count_in, lengths, place, *refs):
    pieces = refs[:count_in]
    (
        x_ref, norm_ref, bias_ref, perm_ref, proj_ref, cos_ref, sin_ref, onehot_ref,
        attn_ref, mixed_ref, a1t_ref, w_ref, wq_ref, wk_ref, qf_ref, kf_ref, v_ref, rden_ref,
        a1, qb, kb, vb, parts, base, first, last, sems,
    ) = refs[count_in:]
    group = pl.program_id(0)

    @pl.when(group == 0)
    def _():
        for unit in range(GROUPS):
            for copy in in_copies(place, pieces, w_ref, sems, unit):
                copy.start()
        def norm_rows(here):
            x = x_ref[here, :].astype(F32)
            centre = x - jnp.mean(x, axis=-1, keepdims=True)
            spread = jnp.mean(centre * centre, axis=-1, keepdims=True)
            a1[here, :] = (
                centre * lax.rsqrt(spread + norm_eps) * norm_ref[0:1, :] + norm_ref[1:2, :]
            ).astype(BF16)

        row_blocks(norm_rows)
        for cols in range(0, D, 256):
            a1t_ref[cols : cols + 256, :] = transposed(a1[:, cols : cols + 256])

    for unit in range(GROUPS):

        @pl.when(group == unit)
        def _():
            for copy in in_copies(place, pieces, w_ref, sems, unit):
                copy.wait()

    count = make_blocks(lengths, base, first, last)
    shard = w_ref.shape[1] // 3
    here = pl.ds(pl.multiple_of(group * shard, 16), shard)
    w = w_ref[:, here, :].reshape(D, D)
    perm = perm_ref[...]
    bias = bias_ref[0]
    proj_both = proj_ref[0]
    proj_high = proj_ref[1, :, :128]
    square = proj_ref[2, :, :128]
    weights = [mm(w[:, WIDTH * i : WIDTH * (i + 1)], perm).astype(BF16) for i in range(2)]

    def feature_rows(here):
        for which, (out_w, out_f, low_f) in enumerate(
            ((wq_ref, qf_ref, qb), (wk_ref, kf_ref, kb))
        ):
            u = (mm(a1[here, :], weights[which]) + bias[which : which + 1, :]) * HD ** (-0.25)
            c = u[:, :128]
            e = u[:, 128:]
            cosine = cos_ref[here, :]
            sine = sin_ref[here, :]
            turned = jnp.concatenate([c * cosine - e * sine, e * cosine + c * sine], axis=1)
            out_w[0, here, :] = turned
            high, low = halves(turned)
            sq_high, sq_low = halves(turned * turned)
            both = mm(high, proj_both)
            logits = (
                both[:, :128] + both[:, 128:] + mm(low, proj_high)
                - (mm(sq_high, square) + mm(sq_low, square))
            )
            phi = jnp.exp(logits) * FEAT ** (-0.5)
            out_f[0, here, :] = phi
            low_f[here, :] = phi.astype(BF16)
        v = mm(a1[here, :], w[:, 2 * WIDTH :]) + bias[2:3, :]
        v_ref[0, here, :] = v
        vb[here, :] = v.astype(BF16)

    row_blocks(feature_rows)
    parts[...] = jnp.zeros_like(parts)

    def one_span(index, carry):
        rows = pl.ds(pl.multiple_of(base[index], 16), SPAN)
        mask = span_mask(onehot_ref, rows, first[index], last[index])
        q = qb[rows, :]
        k = kb[rows, :]
        for pair in range(2):
            v_pair = vb[rows, 128 * pair : 128 * (pair + 1)]
            total = jnp.zeros((SPAN, WIDTH), F32)
            for side in range(2):
                head = 2 * pair + side
                scores = mm_nt(q * lane_mask(32 * head, 32 * head + 32, 128, BF16), k)
                total = total + mm(scores.astype(BF16) * mask, value_rows(v_pair, side))
            parts[pair, rows, :] += total
        return carry

    lax.fori_loop(0, count, one_span, 0)
    for pair in range(2):
        lanes = slice(128 * pair, 128 * (pair + 1))
        inverse = 1.0 / parts[pair, :, 128:]
        rden_ref[0, :, lanes] = inverse
        mixed = parts[pair, :, :128] * inverse
        mixed_ref[0, :, lanes] = mixed
        attn_ref[:, lanes] = mixed.astype(BF16)


def whole_spec(shape, **options):
    return pl.BlockSpec(shape, lambda *_: (0,) * len(shape), **options)


def group_spec(shape):
    return pl.BlockSpec((1,) + shape, lambda g, *_: (g,) + (0,) * len(shape))


def attend(lengths, place, pieces, wide, tokens, norm, bias, perm, proj, cosine, sine, onehot):
    def out(shape, dtype):
        return jax.ShapeDtypeStruct((GROUPS,) + shape, dtype)

    rows_in = 3 * D // wide
    return pl.pallas_call(
        functools.partial(attend_kernel, len(pieces)),
        grid_spec=pltpu.PrefetchScalarGridSpec(
            num_scalar_prefetch=2,
            grid=(GROUPS,),
            in_specs=[any_spec()] * len(pieces)
            + [
                whole_spec((LEN, D)), whole_spec((2, D)), group_spec((3, WIDTH)),
                whole_spec((WIDTH, WIDTH)), whole_spec((3, WIDTH, WIDTH)), whole_spec((LEN, 128)),
                whole_spec((LEN, 128)), whole_spec((LEN, 128)),
            ],
            out_specs=[
                pl.BlockSpec((LEN, WIDTH), lambda g, *_: (0, g)), group_spec((LEN, WIDTH)),
                whole_spec((D, LEN)), whole_spec((wide, rows_in, D)), group_spec((LEN, WIDTH)),
                group_spec((LEN, WIDTH)), group_spec((LEN, 128)), group_spec((LEN, 128)),
                group_spec((LEN, WIDTH)), group_spec((LEN, WIDTH)),
            ],
            scratch_shapes=[
                pltpu.VMEM((LEN, D), BF16),
                pltpu.VMEM((LEN, 128), BF16), pltpu.VMEM((LEN, 128), BF16),
                pltpu.VMEM((LEN, WIDTH), BF16), pltpu.VMEM((2, LEN, WIDTH), F32),
                pltpu.SMEM((32,), jnp.int32), pltpu.SMEM((32,), jnp.int32),
                pltpu.SMEM((32,), jnp.int32), pltpu.SemaphoreType.DMA((GROUPS, 16)),
            ],
        ),
        out_shape=[
            jax.ShapeDtypeStruct((LEN, D), BF16), out((LEN, WIDTH), F32),
            jax.ShapeDtypeStruct((D, LEN), BF16), jax.ShapeDtypeStruct((wide, rows_in, D), BF16),
            out((LEN, WIDTH), F32), out((LEN, WIDTH), F32), out((LEN, 128), F32),
            out((LEN, 128), F32), out((LEN, WIDTH), F32), out((LEN, WIDTH), F32),
        ],
        compiler_params=pltpu.CompilerParams(
            dimension_semantics=("arbitrary",), vmem_limit_bytes=VMEM_LIMIT
        ),
        cost_estimate=cost(20 * 10**9, 40 * 10**6),
        name="attend",
    )(lengths, place, *pieces, tokens, norm, bias, perm, proj, cosine, sine, onehot)


def attend_back_kernel(
    lengths, place, dmixed_ref, mixed_ref, rden_ref, wq_ref, wk_ref, qf_ref, kf_ref, v_ref,
    a1t_ref, w_ref, perm_ref, proj_ref, cos_ref, sin_ref, onehot_ref, ones_ref,
    keep_ref, send_ref, bias_ref, da1_ref,
    qb, kb, dnb, dnh, lift, dqf, dkf, dv, dqkv, base, first, last,
):
    count = make_blocks(lengths, base, first, last)
    qb[...] = qf_ref[0].astype(BF16)
    kb[...] = kf_ref[0].astype(BF16)
    lane = lax.broadcasted_iota(jnp.int32, (1, 128), 1)
    ones = ones_ref[...]
    def lift_rows(here):
        for pair in range(2):
            lanes = slice(128 * pair, 128 * (pair + 1))
            dnum = dmixed_ref[here, lanes] * rden_ref[0, here, lanes]
            high, low = halves(dnum)
            dnb[here, lanes] = high
            part_high, part_low = halves(dnum * mixed_ref[0, here, lanes])
            dden = -mm(jnp.concatenate([part_high, part_low], axis=1), ones)
            den_high, den_low = halves(dden)
            high, low = high.astype(F32), low.astype(F32)
            den_high = pltpu.roll(den_high.astype(F32), 64, 1)
            den_low = pltpu.roll(den_low.astype(F32), 64, 1)
            low_far = pltpu.roll(low, 64, 1)
            v = v_ref[0, here, lanes]
            v_high, v_low = halves(v)
            v_high, v_low = v_high.astype(F32), v_low.astype(F32)
            v_far = pltpu.roll(v_high, 64, 1)
            for side in range(2):
                own = (lane >= 64 * side) & (lane < 64 * side + 64)
                mark = 64 - 64 * side
                rest = jnp.where(lane == mark, den_high, jnp.where(lane == mark + 1, den_low, 0.0))
                both = ((lane == mark) | (lane == mark + 1)).astype(F32)
                head = 2 * pair + side
                dnh[head, here, :128] = jnp.where(own, high, low_far).astype(BF16)
                dnh[head, here, 128:] = jnp.where(own, high, rest).astype(BF16)
                lift[head, here, :128] = jnp.where(own, v_high, v_far).astype(BF16)
                lift[head, here, 128:] = jnp.where(own, v_low, both).astype(BF16)
    row_blocks(lift_rows)
    dqf[...] = jnp.zeros_like(dqf)
    dkf[...] = jnp.zeros_like(dkf)
    dv[...] = jnp.zeros_like(dv)

    def one_span(index, carry):
        rows = pl.ds(pl.multiple_of(base[index], 16), SPAN)
        mask = span_mask(onehot_ref, rows, first[index], last[index])
        q = qb[rows, :]
        k = kb[rows, :]
        q_total = jnp.zeros((SPAN, 128), F32)
        k_total = jnp.zeros((SPAN, 128), F32)
        for pair in range(2):
            lanes = slice(128 * pair, 128 * (pair + 1))
            dn_pair = dnb[rows, lanes]
            v_total = jnp.zeros((SPAN, 128), F32)
            for side in range(2):
                head = 2 * pair + side
                feats = lane_mask(32 * head, 32 * head + 32, 128, BF16)
                q_head = q * feats
                k_head = k * feats
                lifted = lift[head, rows, :]
                dn_head = dnh[head, rows, :]
                scores = mm_nt(k, q_head).astype(BF16) * mask
                dscores = mm_nt(dn_head, lifted).astype(BF16) * mask
                dscores_t = mm_nt(lifted, dn_head).astype(BF16) * mask
                q_total = q_total + mm(dscores, k_head)
                k_total = k_total + mm(dscores_t, q_head)
                own = lane_mask(64 * side, 64 * side + 64, 128, BF16)
                v_total = v_total + mm(scores, dn_pair * own)
            dv[rows, lanes] += v_total
        dqf[rows, :] += q_total
        dkf[rows, :] += k_total
        return carry

    lax.fori_loop(0, count, one_span, 0)
    proj_low = proj_ref[0, :, 128:]
    proj_high = proj_ref[1]
    square = proj_ref[2]
    perm = perm_ref[...]
    def feature_rows(here):
        for which, (w_in, phi_in, dphi) in enumerate(
            ((wq_ref, qf_ref, dqf), (wk_ref, kf_ref, dkf))
        ):
            r = dphi[here, :] * phi_in[0, here, :]
            high, low = halves(r)
            both = jnp.concatenate([high, low], axis=1)
            spread = mm_nt(both, square)
            dw = mm_nt(both, proj_high) + mm_nt(high, proj_low)
            du = (dw - 2.0 * w_in[0, here, :] * spread) * HD ** (-0.25)
            c = du[:, :128]
            e = du[:, 128:]
            cosine = cos_ref[here, :]
            sine = sin_ref[here, :]
            turned = jnp.concatenate([c * cosine + e * sine, e * cosine - c * sine], axis=1)
            dqkv[here, WIDTH * which : WIDTH * (which + 1)] = mm_nt(
                turned.astype(BF16), perm
            ).astype(BF16)

    row_blocks(feature_rows)
    dqkv[:, 2 * WIDTH :] = dv[...].astype(BF16)
    bias_ref[0] = jnp.sum(dqkv[...].astype(F32), axis=0, keepdims=True)
    grad = mm(a1t_ref[...], dqkv[...]).astype(BF16)
    at = pl.program_id(0)
    store_halves(grad, place[3], keep_ref.at[at], send_ref.at[at])
    w = w_ref[...].reshape(D, D)
    fresh = pl.program_id(0) == 0

    @pl.when(fresh)
    def _():
        da1_ref[...] = mm_nt(dqkv[...], w)

    @pl.when(jnp.logical_not(fresh))
    def _():
        da1_ref[...] += mm_nt(dqkv[...], w)


def store_halves(grad, core, keep_ref, send_ref):
    wide, rows = keep_ref.shape[0], D // keep_ref.shape[0]
    half = rows // 2
    parts = grad.reshape(wide, rows, D)
    for cols in range(3):
        block = parts[:, :, WIDTH * cols : WIDTH * (cols + 1)]
        here = pl.ds(half * cols, half)

        @pl.when(core == 0)
        def _():
            keep_ref[:, here, :] = block[:, :half]
            send_ref[:, here, :] = block[:, half:]

        @pl.when(core == 1)
        def _():
            keep_ref[:, here, :] = block[:, half:]
            send_ref[:, here, :] = block[:, :half]


def attend_back(
    lengths, place, wide, dmixed, saved, a1t, w_in, perm, proj, cosine, sine, onehot, ones
):
    mixed, rden, wq, wk, qf, kf, v = saved

    def by_group(shape):
        return pl.BlockSpec((1,) + shape, lambda g, *_: (g,) + (0,) * len(shape))

    rows_in = D // wide
    half = struct((GROUPS, wide, 3 * rows_in // 2, WIDTH), BF16)
    half_spec = once(half.shape)
    if wide > 1:
        half = pltpu.VMEM(half.shape, BF16)
        half_spec = pl.BlockSpec(memory_space=pltpu.VMEM)
    return pl.pallas_call(
        attend_back_kernel,
        grid_spec=pltpu.PrefetchScalarGridSpec(
            num_scalar_prefetch=2,
            grid=(GROUPS,),
            in_specs=[
                pl.BlockSpec((LEN, WIDTH), lambda g, *_: (0, g)),
                by_group((LEN, WIDTH)), by_group((LEN, WIDTH)), by_group((LEN, WIDTH)),
                by_group((LEN, WIDTH)), by_group((LEN, 128)), by_group((LEN, 128)),
                by_group((LEN, WIDTH)), once((D, LEN)),
                pl.BlockSpec((wide, rows_in, D), lambda g, *_: (0, g, 0)),
                once((WIDTH, WIDTH)), once((3, WIDTH, WIDTH)), once((LEN, 128)),
                once((LEN, 128)), once((LEN, 128)), once((WIDTH, 128)),
            ],
            out_specs=[
                half_spec, half_spec, group_spec((1, D)),
                whole_spec((LEN, D)),
            ],
            scratch_shapes=[
                pltpu.VMEM((LEN, 128), BF16), pltpu.VMEM((LEN, 128), BF16),
                pltpu.VMEM((LEN, WIDTH), BF16), pltpu.VMEM((4, LEN, WIDTH), BF16),
                pltpu.VMEM((4, LEN, WIDTH), BF16), pltpu.VMEM((LEN, 128), F32),
                pltpu.VMEM((LEN, 128), F32), pltpu.VMEM((LEN, WIDTH), F32),
                pltpu.VMEM((LEN, D), BF16),
                pltpu.SMEM((32,), jnp.int32), pltpu.SMEM((32,), jnp.int32),
                pltpu.SMEM((32,), jnp.int32),
            ],
        ),
        out_shape=[
            half, half, struct((GROUPS, 1, D), F32), struct((LEN, D), F32),
        ],
        compiler_params=pltpu.CompilerParams(
            dimension_semantics=("arbitrary",), vmem_limit_bytes=BACK_LIMIT
        ),
        cost_estimate=cost(GROUPS * 12 * 10**9, GROUPS * 20 * 10**6),
        name="attend_back",
    )(
        lengths, place, dmixed, mixed, rden, wq, wk, qf, kf, v, a1t, w_in, perm, proj, cosine,
        sine, onehot, ones,
    )


def chunk_step(
    place, wide, bias_up, dy_ref, a2, a2t, dyt, up, down, act, dhidden, y, back, outs, dbias_ref,
    fresh,
):
    rows_up = D // wide
    rows_down = FFC // wide
    dbias_ref[0] = jnp.zeros((1, FFC), F32)

    def chunk_rows(here):
        hidden = mm(a2[here, :], up[...]) + bias_up
        below, density = normal_parts(hidden)
        act_now = (hidden * below).astype(BF16)
        act[here, :] = act_now
        dact = mm_nt(dy_ref[here, :], down[...])
        dhidden_now = (dact * (below + hidden * density)).astype(BF16)
        dhidden[here, :] = dhidden_now
        dbias_ref[0] += jnp.sum(dhidden_now.astype(F32), axis=0, keepdims=True)
        if fresh:
            y[here, :] = mm(act_now, down[...])
            back[here, :] = mm_nt(dhidden_now, up[...])
        else:
            y[here, :] += mm(act_now, down[...])
            back[here, :] += mm_nt(dhidden_now, up[...])

    row_blocks(chunk_rows, True)
    grad_up = mm(a2t[...], dhidden[...]).astype(BF16).reshape(wide, rows_up, FFC)
    grad_down = mm(dyt[...], act[...]).astype(BF16)
    core = place[3]

    def store_up(ref):
        for cols in range(4):
            ref[:, rows_up * cols : rows_up * (cols + 1), :] = grad_up[
                :, :, WIDTH * cols : WIDTH * (cols + 1)
            ]

    def store_down(ref):
        if wide == 1:
            for cols in range(4):
                ref[0, D * cols : D * (cols + 1), :] = grad_down[
                    :, WIDTH * cols : WIDTH * (cols + 1)
                ]
            return
        for shard in range(wide):
            block = grad_down[:, rows_down * shard : rows_down * (shard + 1)]
            ref[shard, :, :128] = block[: D // 2]
            ref[shard, :, 128:] = block[D // 2 :]

    for when, keep_ref, send_ref in outs:
        for side in range(2):
            now = core == side

            @pl.when(now if when is None else now & when)
            def _():
                store_up(keep_ref if side == 0 else send_ref)
                store_down(send_ref if side == 0 else keep_ref)


def load_up(flat, at, up, wide):
    rows = D // wide
    for cols in range(4):
        here = pl.ds(at + rows * cols, rows)
        up[:, WIDTH * cols : WIDTH * (cols + 1)] = flat[:, here, :].reshape(D, WIDTH)


def load_down(flat, at, down, wide):
    rows = FFC // wide
    for cols in range(3):
        here = pl.ds(at + rows * cols, rows)
        down[:, WIDTH * cols : WIDTH * (cols + 1)] = flat[:, here, :].reshape(FFC, WIDTH)


def middle_first_kernel(wide, count_in, place, *refs):
    pieces = refs[:count_in]
    (
        x_ref, attn_ref, dy_ref, rows_ref, bias_up_ref,
        x1_ref, a2_ref, a2t_ref, dyt_ref, y_ref, back_ref, out_ref, keep_ref, send_ref, dbias_ref,
        flat, up, down, act, dhidden, sems,
    ) = refs[count_in:]
    copies = flat_copies(place, pieces, flat, sems)
    for copy in copies:
        copy.start()
    for cols in range(0, D, 256):
        dyt_ref[cols : cols + 256, :] = transposed(dy_ref[:, cols : cols + 256])
    for copy in copies:
        copy.wait()
    half_out = D // wide // 2
    half_flat = flat.shape[1] // 2
    for cols in range(3):
        upper = flat[:, half_out * cols : half_out * (cols + 1), :]
        lower = flat[:, half_flat + half_out * cols : half_flat + half_out * (cols + 1), :]
        out_ref[:, WIDTH * cols : WIDTH * (cols + 1)] = jnp.concatenate(
            [upper, lower], axis=1
        ).reshape(D, WIDTH)
    def norm_rows(here):
        x1 = x_ref[here, :].astype(F32) + (mm(attn_ref[here, :], out_ref[...]) + rows_ref[7:8, :])
        x1_ref[here, :] = x1
        centre = x1 - jnp.mean(x1, axis=-1, keepdims=True)
        spread = jnp.mean(centre * centre, axis=-1, keepdims=True)
        a2_ref[here, :] = (
            centre * lax.rsqrt(spread + norm_eps) * rows_ref[2:3, :] + rows_ref[3:4, :]
        ).astype(BF16)

    row_blocks(norm_rows)
    for cols in range(0, D, 256):
        a2t_ref[cols : cols + 256, :] = transposed(a2_ref[:, cols : cols + 256])
    load_up(flat, 3 * half_out, up, wide)
    load_down(flat, half_flat + 3 * half_out, down, wide)
    chunk_step(
        place, wide, bias_up_ref[0], dy_ref, a2_ref, a2t_ref, dyt_ref, up, down, act, dhidden,
        y_ref, back_ref, [(None, keep_ref, send_ref)], dbias_ref, True,
    )


def middle_rest_kernel(wide, count_in, place, *refs):
    pieces = refs[:count_in]
    (
        dy_ref, a2_ref, a2t_ref, dyt_ref, bias_up_ref, attn_ref, out_ref, rows_ref,
        y_in, back_in, x1_in,
        block_ref, dx1_ref, dmixed_ref, okeep_ref, osend_ref, vec_ref,
        keep_ref, send_ref, dbias_ref,
        flat, up, down, act, dhidden, back, dbranch, sems, flat_sems,
    ) = refs[count_in:]
    step = pl.program_id(0)
    y_copy = pltpu.make_async_copy(y_in, block_ref, sems.at[0])
    back_copy = pltpu.make_async_copy(back_in, back, sems.at[1])
    x1_copy = pltpu.make_async_copy(x1_in, dx1_ref, sems.at[2])

    def chunk_copies(chunk, side):
        if count_in == 1:
            return [
                pltpu.make_async_copy(
                    pieces[0].at[chunk], flat.at[chunk], flat_sems.at[chunk, 0]
                )
            ]
        copies = []
        for flip in range(2):
            column = place[1] if flip == 0 else 1 - place[1]
            for shift in range(4):
                shard = lax.rem(place[0] + 4 - shift, 4) * 2 + column
                copies.append(
                    pltpu.make_async_copy(
                        pieces[2 * side + flip].at[shift], flat.at[chunk, shard],
                        flat_sems.at[chunk, len(copies)],
                    )
                )
        return copies

    def fetch(chunk):
        for side in range(2):

            @pl.when((place[3] == chunk) if side == 0 else (place[3] != chunk))
            def _():
                if side == 0 or count_in > 1:
                    for copy in chunk_copies(chunk, side):
                        copy.start()

    def arrived(chunk):
        for copy in chunk_copies(chunk, 0):
            copy.wait()

    @pl.when(step == 0)
    def _():
        if count_in == 1:
            for chunk in range(2):
                for copy in chunk_copies(chunk, 0):
                    copy.start()
        else:
            fetch(0)
        y_copy.start()
        back_copy.start()
        if count_in > 1:
            fetch(1)
        x1_copy.start()
        arrived(0)
        y_copy.wait()
        back_copy.wait()

    @pl.when(step == 1)
    def _():
        arrived(1)

    load_up(flat.at[step], 0, up, wide)
    load_down(flat.at[step], 4 * (D // wide), down, wide)
    chunk_step(
        place, wide, bias_up_ref[0], dy_ref, a2_ref, a2t_ref, dyt_ref, up, down, act, dhidden,
        block_ref, back, [(None, keep_ref.at[step], send_ref.at[step])], dbias_ref, False,
    )

    @pl.when(step == 1)
    def _():
        x1_copy.wait()
        vec_ref[...] = jnp.zeros_like(vec_ref)

        def last_rows(here):
            x1 = dx1_ref[here, :]
            block_ref[here, :] = x1 + (block_ref[here, :] + rows_ref[8:9, :])
            dn = back[here, :]
            dy = dy_ref[here, :].astype(F32)
            centre = x1 - jnp.mean(x1, axis=-1, keepdims=True)
            spread = jnp.mean(centre * centre, axis=-1, keepdims=True)
            scale = lax.rsqrt(spread + norm_eps)
            zh = centre * scale
            vec_ref[0:1, :] += jnp.sum(dn * zh, axis=0, keepdims=True)
            vec_ref[1:2, :] += jnp.sum(dn, axis=0, keepdims=True)
            e = dn * rows_ref[2:3, :]
            dz = (
                e
                - jnp.mean(e, axis=-1, keepdims=True)
                - zh * jnp.mean(e * zh, axis=-1, keepdims=True)
            ) * scale
            dx1 = dy + dz
            dx1_ref[here, :] = dx1
            low = dx1.astype(BF16)
            dbranch[here, :] = low
            vec_ref[2:3, :] += jnp.sum(low.astype(F32), axis=0, keepdims=True)
            vec_ref[3:4, :] += jnp.sum(dy, axis=0, keepdims=True)
            dmixed_ref[here, :] = mm_nt(low, out_ref[...])

        row_blocks(last_rows, True)
        for cols in range(0, D, 256):
            up[cols : cols + 256, :] = transposed(attn_ref[:, cols : cols + 256])
        store_halves(mm(up[...], dbranch[...]).astype(BF16), place[3], okeep_ref, osend_ref)


def once(shape):
    return whole_spec(shape, pipeline_mode=pl.Buffered(1))


def struct(shape, dtype):
    return jax.ShapeDtypeStruct(shape, dtype)


def weight_scratch():
    return [
        pltpu.VMEM((D, FFC), BF16), pltpu.VMEM((FFC, D), BF16), pltpu.VMEM((LEN, FFC), BF16),
        pltpu.VMEM((LEN, FFC), BF16),
    ]


def middle_first(place, wide, pieces, tokens, attn, cotangent, vectors, bias_up):
    rows_flat = 3 * D // wide + 2 * FFC * D // (WIDTH * wide)
    half = (wide, FFC * D // (WIDTH * wide), WIDTH)
    outs = [
        struct((LEN, D), F32), struct((LEN, D), BF16), struct((D, LEN), BF16),
        struct((D, LEN), BF16), struct((LEN, D), F32), struct((LEN, D), F32),
        struct((D, D), BF16), struct(half, BF16), struct(half, BF16), struct((1, 1, FFC), F32),
    ]
    return pl.pallas_call(
        functools.partial(middle_first_kernel, wide, len(pieces)),
        grid_spec=pltpu.PrefetchScalarGridSpec(
            num_scalar_prefetch=1,
            grid=(1,),
            in_specs=[any_spec()] * len(pieces)
            + [
                once((LEN, D)), once((LEN, D)), once((LEN, D)), once((13, D)),
                pl.BlockSpec((1, 1, FFC), lambda *_: (0, 0, 0)),
            ],
            out_specs=[once(out.shape) for out in outs],
            scratch_shapes=[pltpu.VMEM((wide, rows_flat, WIDTH), BF16)]
            + weight_scratch()
            + [pltpu.SemaphoreType.DMA((16,))],
        ),
        out_shape=outs,
        compiler_params=pltpu.CompilerParams(
            dimension_semantics=("arbitrary",), vmem_limit_bytes=VMEM_LIMIT
        ),
        cost_estimate=cost(14 * 10**9, 30 * 10**6),
        name="middle_first",
    )(place, *pieces, tokens, attn, cotangent, vectors, bias_up)


def middle_rest(place, wide, pieces, cotangent, state, bias_up, attn, w_out, vectors, sums):
    a2, a2t, dyt = state
    half = (wide, FFC * D // (WIDTH * wide), WIDTH)
    out_half = (wide, 3 * D // (2 * wide), WIDTH)
    outs = [
        struct((LEN, D), F32), struct((LEN, D), F32), struct((LEN, D), F32),
        struct(out_half, BF16), struct(out_half, BF16), struct((8, D), F32),
        struct((2,) + half, BF16), struct((2,) + half, BF16), struct((2, 1, FFC), F32),
    ]
    out_specs = [once(out.shape) for out in outs[:8]] + [group_spec((1, FFC))]
    if wide > 1:
        for index in (3, 4, 6, 7):
            outs[index] = pltpu.VMEM(outs[index].shape, BF16)
            out_specs[index] = pl.BlockSpec(memory_space=pltpu.VMEM)
    rows_flat = 2 * FFC * D // (WIDTH * wide)
    return pl.pallas_call(
        functools.partial(middle_rest_kernel, wide, len(pieces)),
        grid_spec=pltpu.PrefetchScalarGridSpec(
            num_scalar_prefetch=1,
            grid=(2,),
            in_specs=[any_spec()] * len(pieces)
            + [
                once((LEN, D)), once((LEN, D)), once((D, LEN)), once((D, LEN)),
                pl.BlockSpec((1, 1, FFC), lambda j, *_: (j + 1, 0, 0)),
                once((LEN, D)), once((D, D)), once((13, D)),
                any_spec(), any_spec(), any_spec(),
            ],
            out_specs=out_specs,
            scratch_shapes=[pltpu.VMEM((2, wide, rows_flat, WIDTH), BF16)]
            + weight_scratch()
            + [
                pltpu.VMEM((LEN, D), F32), pltpu.VMEM((LEN, D), BF16),
                pltpu.SemaphoreType.DMA((3,)), pltpu.SemaphoreType.DMA((2, 8)),
            ],
        ),
        out_shape=outs,
        compiler_params=pltpu.CompilerParams(
            dimension_semantics=("arbitrary",), vmem_limit_bytes=REST_LIMIT
        ),
        cost_estimate=cost(28 * 10**9, 40 * 10**6),
        name="middle_rest",
    )(place, *pieces, cotangent, a2, a2t, dyt, bias_up, attn, w_out, vectors, *sums)


def input_kernel(
    wide, x_ref, dx1_ref, da1_ref, rows_ref, middle_ref, bias_in_ref, bias_first_ref, bias_rest_ref,
    out_ref, vec_ref,
):
    gain = rows_ref[0:1, :]
    x = x_ref[...].astype(F32)
    dn = da1_ref[...]
    centre = x - jnp.mean(x, axis=-1, keepdims=True)
    spread = jnp.mean(centre * centre, axis=-1, keepdims=True)
    scale = lax.rsqrt(spread + norm_eps)
    zh = centre * scale
    e = dn * gain
    dz = (
        e - jnp.mean(e, axis=-1, keepdims=True) - zh * jnp.mean(e * zh, axis=-1, keepdims=True)
    ) * scale
    out_ref[...] = dx1_ref[...] + dz

    @pl.when(pl.program_id(0) == 0)
    def _():
        vec_ref[...] = jnp.zeros_like(vec_ref)
        vec_ref[2:4, :] = middle_ref[0:2, :]
        vec_ref[7:9, :] = middle_ref[2:4, :]
        for group in range(GROUPS):
            lanes = slice(WIDTH * group, WIDTH * (group + 1))
            for which in range(3):
                vec_ref[4 + which : 5 + which, lanes] = bias_in_ref[
                    group, :, WIDTH * which : WIDTH * (which + 1)
                ]
        for chunk in range(CHUNKS):
            for part in range(8):
                value = (
                    bias_first_ref[0] if chunk == 0 else bias_rest_ref[chunk - 1]
                )[:, 128 * part : 128 * (part + 1)]
                start = FFC * chunk + 128 * part if wide == 1 else 384 * part + 128 * chunk
                row, lane = 9 + start // D, start % D
                vec_ref[row : row + 1, lane : lane + 128] = value

    vec_ref[0:1, :] += jnp.sum(dn * zh, axis=0, keepdims=True)
    vec_ref[1:2, :] += jnp.sum(dn, axis=0, keepdims=True)


def input_side(wide, tokens, dx1, da1, vectors, middle_vec, bias_in, bias_first, bias_rest):
    block = pl.BlockSpec((256, D), lambda i: (i, 0))
    return pl.pallas_call(
        functools.partial(input_kernel, wide),
        grid=(LEN // 256,),
        in_specs=[
            block, block, block, whole_spec((13, D)), whole_spec((8, D)),
            whole_spec((GROUPS, 1, D)), whole_spec((1, 1, FFC)), whole_spec((2, 1, FFC)),
        ],
        out_specs=[block, whole_spec((16, D))],
        out_shape=[struct((LEN, D), F32), struct((16, D), F32)],
        compiler_params=pltpu.CompilerParams(dimension_semantics=("arbitrary",)),
        cost_estimate=cost(10**6, 12 * 10**6),
        name="input_side",
    )(tokens, dx1, da1, vectors, middle_vec, bias_in, bias_first, bias_rest)


def tables(lengths, projection):
    ends = jnp.cumsum(lengths[0])
    starts = ends - lengths[0]
    place = jnp.arange(LEN, dtype=jnp.int32)
    member = (place[:, None] >= starts[None, :]) & (place[:, None] < ends[None, :])
    offset = jnp.sum(jnp.where(member, starts[None, :], 0), axis=1)
    position = (place - offset).astype(F32)
    freq = 10000.0 ** (-jnp.arange(32, dtype=F32) / 32)
    angles = position[:, None] * jnp.tile(freq, 4)[None, :]
    onehot = jnp.pad(member.astype(BF16), ((0, 0), (0, 128 - member.shape[1])))
    eye = jnp.asarray(np.eye(4, dtype=np.float32))
    lifted = jnp.einsum("hif,ab->haibf", projection.reshape(2, 32, FEAT), eye)
    lifted = lifted.reshape(WIDTH, 128)
    rounded = lax.reduce_precision(lifted, 8, 7)
    high, low = rounded.astype(BF16), (lifted - rounded).astype(BF16)
    square = np.zeros((2, 4, 32, 4, 32), np.float32)
    for head in range(4):
        square[:, head, :, head, :] = 0.5
    square = jnp.asarray(square.reshape(WIDTH, 128), BF16)
    proj = jnp.stack(
        [
            jnp.concatenate([high, low], axis=1),
            jnp.concatenate([high, high], axis=1),
            jnp.concatenate([square, square], axis=1),
        ]
    )
    return jnp.cos(angles), jnp.sin(angles), onehot, proj


def wide_perm(shift_z, flip_x):
    pairs = []
    for z in range(4):
        for x in range(2):
            target_x = 1 - x if flip_x else x
            pairs.append((2 * z + x, 2 * ((z + shift_z) % 4) + target_x))
    return pairs


def narrow_perm(flip_y, flip_core):
    pairs = []
    for y in range(2):
        for core in range(2):
            pairs.append(
                (2 * y + core, 2 * (1 - y if flip_y else y) + (1 - core if flip_core else core))
            )
    return pairs


def over_z(values, shift):
    return lax.ppermute(values, "wide", wide_perm(shift, False))


def over_x(values):
    return lax.ppermute(values, "wide", wide_perm(0, True))


def over_far(values, bit):
    return lax.ppermute(values, "wide", [(w, w ^ bit) for w in range(8)])


def over_y(values):
    return lax.ppermute(values, "narrow", narrow_perm(True, False))


def over_core(values):
    return lax.ppermute(values, "narrow", narrow_perm(False, True))


def tie(*values):
    return lax.optimization_barrier(values)


def special():
    return lax.axis_size("wide") == 8 and lax.axis_size("narrow") == 4


def sum_wide(values):
    if not special():
        return lax.psum(values, "wide")
    for perm in (wide_perm(0, True), [(w, w ^ 2) for w in range(8)], [(w, w ^ 4) for w in range(8)]):
        values = values + lax.ppermute(values, "wide", perm)
    return values


def sum_narrow(values):
    if not special():
        return lax.psum(values, "narrow")
    pair = values + over_core(values)
    return pair + over_y(pair)


def along_z(mine):
    return jnp.stack([mine] + [over_z(mine, shift) for shift in (1, 2, 3)])


def small_call(kernel, name, place, operands, outs):
    return pl.pallas_call(
        kernel,
        grid_spec=pltpu.PrefetchScalarGridSpec(
            num_scalar_prefetch=1,
            grid=(1,),
            in_specs=[once(value.shape) for value in operands],
            out_specs=[once(out.shape) for out in outs],
        ),
        out_shape=outs,
        compiler_params=pltpu.CompilerParams(
            dimension_semantics=("arbitrary",), vmem_limit_bytes=VMEM_LIMIT
        ),
        cost_estimate=cost(10**6, sum(4 * math.prod(v.shape) for v in operands + outs)),
        name=name,
    )(place, *operands)


def held_call(kernel, name, place, operands, outs, held=None, flops=10**6):
    here = pl.BlockSpec(memory_space=pltpu.VMEM)
    held = len(outs) if held is None else held
    return pl.pallas_call(
        kernel,
        in_specs=[pl.BlockSpec(memory_space=pltpu.SMEM)] + [here] * len(operands),
        out_specs=[here] * len(outs),
        out_shape=[
            pltpu.VMEM(out.shape, out.dtype) if index < held else out
            for index, out in enumerate(outs)
        ],
        compiler_params=pltpu.CompilerParams(vmem_limit_bytes=24 * 1024 * 1024),
        cost_estimate=pl.CostEstimate(flops=flops, transcendentals=0, bytes_accessed=10**5),
        name=name,
    )(place, *[pltpu.with_memory_space_constraint(value, pltpu.VMEM) for value in operands])


def pick_kernel(
    place, in_ref, out_ref, up_ref, down_ref, near_ref, last_ref, first_ref, rest_ref
):
    core = place[3]
    here = pl.ds(pl.multiple_of(48 * core, 16), 48)
    for group in range(GROUPS):
        ref, index = (near_ref, group) if group < 2 else (last_ref, 0)
        for which in range(3):
            ref[index, :, WIDTH * which : WIDTH * (which + 1)] = in_ref[
                which, here, WIDTH * group : WIDTH * (group + 1)
            ].astype(BF16)
    for cols in range(3):
        first_ref[48 * cols : 48 * (cols + 1), :] = out_ref[
            here, WIDTH * cols : WIDTH * (cols + 1)
        ].astype(BF16)

    def put_up(ref, at, chunk):
        for cols in range(4):
            rows = slice(at + 96 * cols, at + 96 * (cols + 1))
            for side in range(2):
                start = 384 * (2 * cols + side) + 128 * chunk
                ref[rows, 128 * side : 128 * (side + 1)] = up_ref[:, start : start + 128].astype(
                    BF16
                )

    def put_down(ref, at, chunk):
        for cols in range(3):
            ref[at + 128 * cols : at + 128 * (cols + 1), :] = down_ref[
                128 * chunk : 128 * (chunk + 1), WIDTH * cols : WIDTH * (cols + 1)
            ].astype(BF16)

    for side in range(2):

        @pl.when(core == side)
        def _():
            if side == 0:
                put_up(first_ref, 144, 0)
            else:
                put_down(first_ref, 144, 0)

        @pl.when(core == side)
        def _():
            put_up(rest_ref, 0, 1 + side)
            put_down(rest_ref, 384, 1 + side)


def chunk_of(ref, chunk, shard):
    return ref[chunk, shard] if len(ref.shape) == 4 else ref[shard]


def first_sum_kernel(place, *refs):
    send_ref, keep_ref = refs[-2:]
    x = place[1]
    at = 0
    for index in range(0, len(refs) - 2, 2):
        own, got = refs[index], refs[index + 1]
        for part in range(own.shape[0] if len(own.shape) == 4 and own.shape[0] == 3 else 1):
            rows = own.shape[-2]
            here = pl.ds(at, rows)
            for z in range(4):
                for out, side in ((keep_ref, x), (send_ref, 1 - x)):
                    out[z, here, :] = (
                        chunk_of(own, part, 2 * z + side).astype(F32)
                        + chunk_of(got, part, 2 * z + side).astype(F32)
                    ).astype(BF16)
            at += rows


def first_sum(place, pairs):
    rows = sum(
        own.shape[-2] * (own.shape[0] if own.ndim == 4 and own.shape[0] == 3 else 1)
        for own, _ in pairs
    )
    return held_call(
        first_sum_kernel, "first_sum", place, [value for pair in pairs for value in pair],
        [struct((4, rows, WIDTH), BF16)] * 2,
    )


def first_sum_y_kernel(place, own, got, send, keep):
    y = place[2]
    for group in range(GROUPS):
        here = pl.ds(144 * group, 144)
        for shard in range(8):
            total = own[group, shard].astype(F32) + got[group, shard].astype(F32)
            left, right = total[:, :128].astype(BF16), total[:, 128:].astype(BF16)
            keep[shard, here, :] = jnp.where(y == 0, left, right)
            send[shard, here, :] = jnp.where(y == 0, right, left)


def split_x_kernel(place, own, got, send, keep):
    x = place[1]
    for z in range(4):
        for out, side in ((keep, x), (send, 1 - x)):
            out[z] = (own[2 * z + side].astype(F32) + got[2 * z + side].astype(F32)).astype(BF16)


def second_sum_kernel(place, own_ref, got_ref, *outs):
    z = place[0]
    for shift, out in enumerate(outs):
        there = lax.rem(z + shift, 4)
        out[...] = (own_ref[there].astype(F32) + got_ref[there].astype(F32)).astype(BF16)


def second_sum(place, own, got):
    outs = [struct(own.shape[1:], BF16)] * 4
    return held_call(second_sum_kernel, "second_sum", place, [own, got], outs)


def z_sum_kernel(place, *refs):
    total = refs[0][...].astype(F32)
    for ref in refs[1:4]:
        total = total + ref[...].astype(F32)
    rows = refs[0].shape[0]
    refs[-1][:rows, :] = total.astype(refs[-1].dtype)
    if len(refs) == 7:
        refs[-1][rows:, :] = (refs[4][...].astype(F32) + refs[5][...].astype(F32)).astype(BF16)


def z_sum(place, parts, below=(), got=None):
    if got is None:
        got = [over_z(parts[shift], shift) for shift in (1, 2, 3)]
    rows = parts[0].shape[0] + (below[0].shape[0] if below else 0)
    return held_call(
        z_sum_kernel, "z_sum", place, [parts[0]] + got + list(below),
        [struct((rows, parts[0].shape[1]), BF16 if below else F32)],
        flops=3 * 10**10 if below else 10**6,
    )[0]


def first_sum_z_kernel(place, *refs):
    z = place[0]
    outs = refs[-4:]
    for shift, out in enumerate(outs):
        there = lax.rem(z + shift, 4) * 2
        at = 0
        for index in range(0, len(refs) - 4, 2):
            own, got = refs[index], refs[index + 1]
            rows = own.shape[-2]
            for x in range(2):
                out[x, at : at + rows, :] = (
                    chunk_of(own, 1, there + x).astype(F32)
                    + chunk_of(got, 1, there + x).astype(F32)
                ).astype(BF16)
            at += rows


def first_sum_z(place, pairs):
    rows = sum(own.shape[-2] for own, _ in pairs)
    return held_call(
        first_sum_z_kernel, "first_sum_z", place, [value for pair in pairs for value in pair],
        [struct((2, rows, WIDTH), BF16)] * 4,
    )


def split_sum_kernel(place, *refs):
    keep, send = refs[-2:]
    x = place[1]
    for out, at in ((keep, x), (send, 1 - x)):
        total = refs[0][at].astype(F32)
        for ref in refs[1:4]:
            total = total + ref[at].astype(F32)
        out[...] = total.astype(BF16)


def split_sum(place, parts):
    return held_call(
        split_sum_kernel, "split_sum", place, parts, [struct(parts[0].shape[1:], BF16)] * 2
    )


def to_row(column):
    size = column.shape[0]
    eye = lax.broadcasted_iota(jnp.int32, (size, size), 0) == lax.broadcasted_iota(
        jnp.int32, (size, size), 1
    )
    return jnp.sum(jnp.where(eye, column, 0.0), axis=0, keepdims=True)


def to_column(row):
    size = row.shape[1]
    eye = lax.broadcasted_iota(jnp.int32, (size, size), 0) == lax.broadcasted_iota(
        jnp.int32, (size, size), 1
    )
    return jnp.sum(jnp.where(eye, row, 0.0), axis=1, keepdims=True)


DECAY = 1.0 - STEP ** (-0.8)


def lane_values(values):
    lane = lax.broadcasted_iota(jnp.int32, (1, D), 1)
    row = jnp.zeros((1, D), F32)
    for index, value in enumerate(values):
        row = jnp.where(lane == index, value, row)
    return row


def moments(grad, rows_old):
    plain = grad * grad
    squares = plain + square_eps
    mean = jnp.sum(squares, axis=1, keepdims=True) * (1.0 / grad.shape[1])
    rows_new = DECAY * rows_old + (1.0 - DECAY) * to_row(mean)
    total = jnp.sum(rows_new, axis=1, keepdims=True)
    divided = jnp.sum(plain * to_column(1.0 / rows_new), axis=0, keepdims=True)
    return rows_new, total, jnp.sum(squares, axis=0, keepdims=True), divided


def ffn_moments_kernel(
    place, own, got, up_rows, down_rows, out_rows,
    up_grad, down_grad, out_grad, up_rows_new, down_rows_new, out_rows_new, sums,
):
    core = place[3]

    def collect(low, high):
        for chunk in range(CHUNKS):
            at = 384 * chunk
            for cols in range(4):
                for side in range(2):
                    start = 384 * (2 * cols + side) + 128 * chunk
                    up_grad[:, start : start + 128] = low[
                        at + 96 * cols : at + 96 * (cols + 1), 128 * side : 128 * (side + 1)
                    ]
            for side in range(2):
                down_grad[128 * chunk : 128 * (chunk + 1), 384 * side : 384 * (side + 1)] = (
                    jnp.transpose(high[at : at + 384, 128 * side : 128 * (side + 1)])
                )
        for cols in range(3):
            lanes = slice(WIDTH * cols, WIDTH * (cols + 1))
            at = 1152 + 48 * cols
            out_grad[:48, lanes] = low[at : at + 48, :]
            out_grad[48:, lanes] = high[at : at + 48, :]

    @pl.when(core == 0)
    def _():
        collect(own, got)

    @pl.when(core == 1)
    def _():
        collect(got, own)

    up_new, up_total, up_sums, up_divided = moments(up_grad[...], up_rows[...])
    down_new, down_total, down_sums, down_divided = moments(down_grad[...], down_rows[...])
    out_new, out_total, out_sums, out_divided = moments(out_grad[...], out_rows[...])
    up_rows_new[...] = up_new
    down_rows_new[...] = down_new
    out_rows_new[...] = out_new
    for part in range(4):
        lanes = slice(D * part, D * (part + 1))
        sums[part : part + 1, :] = up_sums[:, lanes]
        sums[4 + part : 5 + part, :] = up_divided[:, lanes]
    sums[8:9, :] = down_sums
    sums[9:10, :] = down_divided
    sums[10:11, :] = out_sums
    sums[11:12, :] = out_divided
    sums[12:13, :] = lane_values([up_total, down_total, out_total])
    sums[13:16, :] = jnp.zeros((3, D), F32)


def in_moments_kernel(
    place, own, own_y, other, other_y, rows_old, vector, vector_far, ffn_sums, grad, rows_new,
    sums,
):
    def collect(low, high):
        for group in range(GROUPS):
            for which in range(3):
                rows = slice(144 * group + 48 * which, 144 * group + 48 * (which + 1))
                for side in range(2):
                    start = WIDTH * group + 128 * side
                    grad[which, :48, start : start + 128] = low[side][rows, :]
                    grad[which, 48:, start : start + 128] = high[side][rows, :]

    for core in range(2):
        for y in range(2):

            @pl.when((place[3] == core) & (place[2] == y))
            def _():
                mine = (own, own_y) if y == 0 else (own_y, own)
                far = (other, other_y) if y == 0 else (other_y, other)
                collect(mine if core == 0 else far, far if core == 0 else mine)

    totals = []
    for which in range(3):
        new, total, columns, divided = moments(grad[which], rows_old[which : which + 1, :])
        rows_new[which : which + 1, :] = new
        sums[which : which + 1, :] = columns
        sums[3 + which : 4 + which, :] = divided
        totals.append(total)
    sums[6:7, :] = lane_values(totals)
    sums[7:8, :] = jnp.zeros((1, D), F32)
    sums[8:24, :] = vector[...] + vector_far[...]
    sums[24:40, :] = ffn_sums[...]


def matrix_step(weight, grad, rows, cols, total, col_sums, divided, rows_full, rate):
    cols_new = DECAY * cols + (1.0 - DECAY) * col_sums * (1.0 / rows_full)
    mean = total * (1.0 / rows_full)
    square_sum = mean * jnp.sum(divided / cols_new, axis=1, keepdims=True)
    rms = jnp.sqrt(square_sum * (1.0 / (rows_full * grad.shape[1])))
    factor = to_column(lax.rsqrt(rows / mean)) * (rate / jnp.maximum(1.0, rms / clip_level))
    return cols_new, weight - grad * factor * lax.rsqrt(cols_new)


def finish_kernel(
    place, inward, up, down, out, in_grad, up_grad, down_grad, out_grad, in_rows, up_rows,
    down_rows, out_rows, in_cols, up_cols, down_cols, out_cols, sums, vectors, vector_state,
    in_cols_new, up_cols_new, down_cols_new, out_cols_new, in_next, up_next, down_next, out_next,
    vector_grad, state_next, vectors_next,
):
    base_rate = 0.3 * D ** (-0.5)
    for which in range(3):
        here = slice(which, which + 1)
        in_cols_new[here, :], in_next[which] = matrix_step(
            inward[which], in_grad[which], in_rows[here, :], in_cols[here, :],
            sums[6:7, which : which + 1], sums[here, :], sums[3 + which : 4 + which, :], D,
            base_rate,
        )

    def wide_row(first):
        return jnp.concatenate([sums[first + i : first + i + 1, :] for i in range(4)], axis=1)

    up_new, up_next[...] = matrix_step(
        up[...], up_grad[...], up_rows[...], up_cols[...], sums[36:37, 0:1], wide_row(24),
        wide_row(28), D, base_rate,
    )
    down_new, down_next[...] = matrix_step(
        down[...], down_grad[...], down_rows[...], down_cols[...], sums[36:37, 1:2],
        sums[32:33, :], sums[33:34, :], FF, 0.3 * FF ** (-0.5),
    )
    out_new, out_next[...] = matrix_step(
        out[...], out_grad[...], out_rows[...], out_cols[...], sums[36:37, 2:3],
        sums[34:35, :], sums[35:36, :], D, 1.2 * D ** (-0.5),
    )
    up_cols_new[...] = up_new.reshape(FF)
    down_cols_new[...] = down_new.reshape(D)
    out_cols_new[...] = out_new.reshape(D)
    g = sums[8:21, :]
    vector_grad[...] = g
    state = DECAY * vector_state[...] + (1.0 - DECAY) * (g * g + square_eps)
    state_next[...] = state
    update = g * lax.rsqrt(state)
    total = jnp.sum(jnp.sum(update * update, axis=0, keepdims=True), axis=1, keepdims=True)
    rms = jnp.sqrt(total * (1.0 / (13 * D)))
    vectors_next[...] = vectors[...] - update * (0.25 / jnp.maximum(1.0, rms / clip_level))


def shards(
    tokens, cotangent, lengths, projection, inward, outward, expand, shrink, vectors,
    inward_rows, inward_columns, outward_rows, outward_columns, expand_rows, expand_columns,
    shrink_rows, shrink_columns, vector_state,
):
    full = special()
    rows = outward.shape[0]
    wide = 8 if full else 1
    wide_at = lax.axis_index("wide").astype(jnp.int32)
    narrow_at = lax.axis_index("narrow").astype(jnp.int32)
    core = narrow_at % 2 if full else jnp.int32(0)
    place = jnp.stack([wide_at // 2, wide_at % 2, narrow_at // 2, core])
    per = FFC // wide
    cosine, sine, onehot, proj = tables(lengths, projection)
    if full:
        *own_in, own_first, own_rest = small_call(
            pick_kernel, "pick", place, [inward, outward, expand, shrink],
            [
                struct((2, 48, D), BF16), struct((1, 48, D), BF16), struct((528, WIDTH), BF16),
                struct((768, WIDTH), BF16),
            ],
        )
        in_z = [along_z(value) for value in own_in]
        *in_z, own_first, cosine, sine, onehot, proj = tie(
            *in_z, own_first, cosine, sine, onehot, proj
        )
        first_z = along_z(own_first)
        in_x = [over_x(value) for value in in_z]
        pieces_in = []
        *in_z, first_z = tie(*in_z, *in_x, first_z)
        for near, far in zip(in_z[:2], in_z[2:]):
            pieces_in += [near, far, over_core(near), over_core(far)]
        *pieces_in, first_z, own_rest = tie(*pieces_in, first_z, own_rest)
        first_x = over_x(first_z)
        rest_got = [over_z(own_rest, shift) for shift in (1, 2, 3)]
    else:
        in_low = lax.all_gather(inward.astype(BF16), "wide", axis=1, tiled=True)
        out_low = lax.all_gather(outward.astype(BF16), "wide", axis=0, tiled=True)
        up_low = lax.all_gather(expand.astype(BF16), "wide", axis=0, tiled=True)
        down_low = lax.all_gather(shrink.astype(BF16), "wide", axis=0, tiled=True)
        units = jnp.transpose(in_low.reshape(3, D, GROUPS, WIDTH), (2, 1, 0, 3))
        pieces_in = [units.reshape(1, 3 * D, D)]

        def blocks(matrix):
            count = matrix.shape[1] // WIDTH
            return jnp.transpose(matrix.reshape(-1, count, WIDTH), (1, 0, 2)).reshape(-1, WIDTH)

        ups = [blocks(up_low[:, FFC * j : FFC * (j + 1)]) for j in range(CHUNKS)]
        downs = [blocks(down_low[FFC * j : FFC * (j + 1)]) for j in range(CHUNKS)]
        half = D // 2
        pieces_first = [
            jnp.concatenate([blocks(out_low[:half]), ups[0], blocks(out_low[half:]), downs[0]])[
                None
            ]
        ]
        pieces_rest = [
            jnp.stack([jnp.concatenate([ups[j], downs[j]])[None] for j in range(1, CHUNKS)])
        ]
    perm = jnp.asarray(head_perm(), BF16)
    block_ones = np.kron(np.eye(2, dtype=np.float32), np.ones((64, 64), np.float32))
    ones = jnp.asarray(np.concatenate([block_ones, block_ones]), BF16)
    split = vectors[4:6].reshape(2, GROUPS, 4, 2, 32)
    bias_qk = jnp.transpose(split, (0, 1, 3, 2, 4)).reshape(2, GROUPS, WIDTH)
    bias = jnp.concatenate([bias_qk, vectors[6].reshape(1, GROUPS, WIDTH)])
    bias = jnp.transpose(bias, (1, 0, 2))
    bias_up = vectors[9:].reshape(wide, CHUNKS, per)
    bias_up = jnp.transpose(bias_up, (1, 0, 2)).reshape(CHUNKS, 1, FFC)
    attn, mixed, a1t, w_in, wq, wk, qf, kf, v, rden = attend(
        lengths, place, pieces_in, wide, tokens, vectors[:2], bias, perm, proj, cosine, sine,
        onehot,
    )
    if full:
        attn, first_x, *rest_got = tie(attn, first_x, *rest_got)
        rest_z = jnp.stack([own_rest] + rest_got)
        first_cores = [over_core(first_z), over_core(first_x)]
        *first_cores, rest_z = tie(*first_cores, rest_z)
        pieces_first = [first_z, first_x] + first_cores
        rest_x = over_x(rest_z)
    x1, a2, a2t, dyt, y, back, w_out, keep0, send0, dbias0 = middle_first(
        place, wide, pieces_first, tokens, attn, cotangent, vectors, bias_up
    )
    if full:
        rest_core = over_core(rest_z)
        rest_x, rest_core, send0, y = tie(rest_x, rest_core, send0, y)
        pieces_rest = [rest_z, rest_x, rest_core, over_core(rest_x)]
        got0 = over_core(send0)
    (
        block_out, dx1, dmixed, okeep, osend, middle_vec, keep12, send12, dbias12,
    ) = middle_rest(
        place, wide, pieces_rest, cotangent, (a2, a2t, dyt), bias_up, attn, w_out, vectors,
        (y, back, x1),
    )
    if full:
        got0, send12, osend = tie(got0, send12, osend)
        got12 = over_core(send12)
        send_b, keep_b = first_sum(place, [(keep0, got0), (keep12, got12)])
        e_parts = first_sum_z(place, [(keep12, got12), (okeep, over_core(osend))])
        dmixed, send_b, keep_b, *e_parts = tie(dmixed, send_b, keep_b, *e_parts)
        got_b = over_x(send_b)
        e_got = [over_z(e_parts[shift], shift) for shift in (1, 2, 3)]
    saved = (mixed, rden, wq, wk, qf, kf, v)
    in_keep, in_send, in_bias, da1 = attend_back(
        lengths, place, wide, dmixed, saved, a1t, w_in, perm, proj, cosine, sine, onehot, ones
    )
    if full:
        b_parts = list(second_sum(place, keep_b, got_b))
        in_send, da1, *e_got, b_parts[1] = tie(in_send, da1, *e_got, b_parts[1])
        keep_e, send_e = split_sum(place, [e_parts[0]] + e_got)
        send_e, in_send = tie(send_e, in_send)
        got_e = over_x(send_e)
        got_in = over_core(in_send)
        send_c, keep_c = held_call(
            first_sum_y_kernel, "first_sum_y", place, [in_keep, got_in],
            [struct((8, 432, 128), BF16)] * 2,
        )
        da1, send_c = tie(da1, send_c)
        got_c = over_y(send_c)
    input_grad, vector_local = input_side(
        wide, tokens, dx1, da1, vectors, middle_vec, in_bias, dbias0, dbias12
    )
    if full:
        def pair_sum(mine, got):
            half_sum = mine.astype(F32) + got.astype(F32)
            return half_sum, over_core(half_sum)

        got_c, input_grad, vector_local = tie(got_c, input_grad, vector_local)
        send_c, keep_c = held_call(
            split_x_kernel, "split_x", place, [keep_c, got_c], [struct((4, 432, 128), BF16)] * 2
        )
        send_c, b_parts[0] = tie(send_c, b_parts[0])
        got_c = over_x(send_c)
        ffn_mine = z_sum(place, b_parts, (keep_e, got_e))
        ffn_mine, got_c = tie(ffn_mine, got_c)
        c_parts = second_sum(place, keep_c, got_c)
        ffn_mine, *c_parts = tie(ffn_mine, *c_parts)
        ffn_y = over_y(ffn_mine)
        c_mine = z_sum(place, c_parts)
        c_mine, vector_local = tie(c_mine, vector_local)
        c_y = over_y(c_mine)
        c_y, vector_y = tie(c_y, over_y(vector_local))
        vector_pair = vector_local + vector_y
        c_core = over_core(c_mine)
        ffn_y, c_mine = tie(ffn_y, c_mine)
        ffn_own, ffn_got = pair_sum(ffn_mine, ffn_y)
        expand_grad, shrink_grad, outward_grad, up_rows, down_rows, out_rows, sums = held_call(
            ffn_moments_kernel, "ffn_moments", place,
            [
                ffn_own, ffn_got, expand_rows[None], shrink_rows[None], outward_rows[None],
            ],
            [
                struct(expand.shape, F32), struct(shrink.shape, F32), struct(outward.shape, F32),
                struct((1, 96), F32), struct((1, 384), F32), struct((1, 96), F32),
                struct((16, D), F32),
            ],
            0,
        )
        c_y, sums = tie(c_y, sums)
        inward_grad, in_rows, sums = held_call(
            in_moments_kernel, "in_moments", place,
            [
                c_mine, c_y, c_core, over_core(c_y), inward_rows, vector_pair,
                over_core(vector_pair), sums,
            ],
            [struct(inward.shape, F32), struct((3, 96), F32), struct((40, D), F32)],
            0,
        )
        sums = sum_wide(sums)
        (
            in_cols, up_cols, down_cols, out_cols, inward_next, expand_next, shrink_next,
            outward_next, vector_grad, vector_state_next, vectors_next,
        ) = small_call(
            finish_kernel, "finish", place,
            [
                inward, expand, shrink, outward, inward_grad, expand_grad, shrink_grad,
                outward_grad, in_rows, up_rows, down_rows, out_rows, inward_columns,
                expand_columns[None], shrink_columns[None], outward_columns[None], sums, vectors,
                vector_state,
            ],
            [
                struct((3, D), F32), struct((FF,), F32), struct((D,), F32),
                struct((D,), F32), struct(inward.shape, F32), struct(expand.shape, F32),
                struct(shrink.shape, F32), struct(outward.shape, F32), struct((13, D), F32),
                struct((13, D), F32), struct((13, D), F32),
            ],
        )
        return (
            block_out, input_grad, inward_grad, outward_grad, expand_grad, shrink_grad,
            vector_grad, in_rows, in_cols, out_rows[0], out_cols, up_rows[0], up_cols,
            down_rows[0], down_cols, vector_state_next, inward_next, outward_next,
            expand_next, shrink_next, vectors_next,
        )
    vector_part = sum_narrow(vector_local[:13])

    def reduced(values, axis):
        part = lax.psum_scatter(values, "wide", scatter_dimension=axis, tiled=True)
        return lax.psum(part.astype(F32), "narrow")

    keeps = [keep0, keep12[0], keep12[1]]
    sends = [send0, send12[0], send12[1]]
    up_grads = [
        jnp.transpose(keep.reshape(4, D, WIDTH), (1, 0, 2)).reshape(D, FFC) for keep in keeps
    ]
    down_grads = [
        jnp.transpose(send.reshape(4, D, WIDTH), (0, 2, 1)).reshape(FFC, D) for send in sends
    ]
    expand_grad = reduced(jnp.concatenate(up_grads, axis=1), 0)
    shrink_grad = reduced(jnp.concatenate(down_grads, axis=0), 0)

    def rebuilt(keep, send):
        return jnp.concatenate(
            [keep.reshape(-1, 3, D // 2, WIDTH), send.reshape(-1, 3, D // 2, WIDTH)], axis=2
        )

    outward_grad = reduced(jnp.transpose(rebuilt(okeep, osend)[0], (1, 0, 2)).reshape(D, D), 0)
    in_units = rebuilt(in_keep, in_send)
    inward_grad = reduced(jnp.transpose(in_units, (1, 2, 0, 3)).reshape(3, D, D), 1)
    decay = 1.0 - STEP ** (-0.8)
    wide_count = lax.axis_size("wide")
    grads_list = [inward_grad, outward_grad[None], expand_grad[None], shrink_grad[None]]
    rows_old = [inward_rows, outward_rows[None], expand_rows[None], shrink_rows[None]]
    columns_old = [
        inward_columns,
        outward_columns[None],
        expand_columns[None],
        shrink_columns[None],
    ]
    weights_old = [inward, outward[None], expand[None], shrink[None]]
    rates = [0.3 * D ** (-0.5), 1.2 * D ** (-0.5), 0.3 * D ** (-0.5), 0.3 * FF ** (-0.5)]
    bounds = [0, 3, 4, 5, 6]
    rows_next = []
    column_parts = []
    for member in range(4):
        squares = grads_list[member] * grads_list[member] + square_eps
        rows_next.append(decay * rows_old[member] + (1.0 - decay) * jnp.mean(squares, axis=-1))
        column_parts.append(jnp.sum(squares, axis=-2))
    row_totals = jnp.concatenate([jnp.sum(entry, axis=-1) for entry in rows_next])
    shapes = [part.shape for part in column_parts] + [row_totals.shape, vector_part.shape]
    flat = jnp.concatenate(
        [part.reshape(-1) for part in column_parts + [row_totals, vector_part]]
    )
    flat = jnp.pad(flat, (0, -flat.shape[0] % 1024)).reshape(-1, 128)
    flat = sum_wide(flat).reshape(-1)
    summed = []
    offset = 0
    for shape in shapes:
        size = 1
        for extent in shape:
            size *= extent
        summed.append(flat[offset : offset + size].reshape(shape))
        offset += size
    column_sums = list(summed[0:4])
    totals_sum = summed[4]
    vector_grad = summed[5]
    columns_next = []
    scaled_list = []
    row_means = []
    sizes_full = []
    for member in range(4):
        grad_now = grads_list[member]
        rows_full = grad_now.shape[-2] * wide_count
        sizes_full.append(rows_full * grad_now.shape[-1])
        columns_next.append(
            decay * columns_old[member] + (1.0 - decay) * column_sums[member] / rows_full
        )
        row_mean = totals_sum[bounds[member] : bounds[member + 1]] / rows_full
        row_means.append(row_mean)
        scaled_list.append(
            grad_now
            * lax.rsqrt(rows_next[member] / row_mean[:, None])[..., None]
            * lax.rsqrt(columns_next[member])[:, None, :]
        )
    partial_squares = jnp.concatenate(
        [jnp.sum(entry * entry, axis=(-2, -1)) for entry in scaled_list]
    )
    total_squares = sum_wide(jnp.pad(partial_squares, (0, 122)).reshape(1, 128))[0, :6]
    rms_list = [
        jnp.sqrt(total_squares[bounds[member] : bounds[member + 1]] / sizes_full[member])
        for member in range(4)
    ]
    weights_next = []
    for member in range(4):
        limiter = jnp.maximum(1.0, rms_list[member] / clip_level)
        weights_next.append(
            weights_old[member] - rates[member] * scaled_list[member] / limiter[:, None, None]
        )
    vector_state_next = decay * vector_state + (1.0 - decay) * (
        vector_grad * vector_grad + square_eps
    )
    vector_update = vector_grad * lax.rsqrt(vector_state_next)
    vector_rms = jnp.sqrt(jnp.mean(vector_update * vector_update))
    vectors_next = vectors - 0.25 * vector_update / jnp.maximum(1.0, vector_rms / clip_level)
    return (
        block_out,
        input_grad,
        inward_grad,
        outward_grad,
        expand_grad,
        shrink_grad,
        vector_grad,
        rows_next[0],
        columns_next[0],
        rows_next[1][0],
        columns_next[1][0],
        rows_next[2][0],
        columns_next[2][0],
        rows_next[3][0],
        columns_next[3][0],
        vector_state_next,
        weights_next[0],
        weights_next[1][0],
        weights_next[2][0],
        weights_next[3][0],
        vectors_next,
    )


def solution(mesh):
    placed = (
        P(("narrow", "wide"), None),
        P(("narrow", "wide"), None),
        P(("narrow", "wide"), None),
        P(),
        P(None, "wide", None),
        P("wide", None),
        P("wide", None),
        P("wide", None),
        P(),
        P(None, "wide"),
        P(),
        P("wide"),
        P(),
        P("wide"),
        P(),
        P("wide"),
        P(),
        P(),
    )
    return jax.shard_map(
        shards,
        mesh=mesh,
        in_specs=placed,
        out_specs=(
            P(("narrow", "wide"), None),
            P(("narrow", "wide"), None),
            P(None, "wide", None),
            P("wide", None),
            P("wide", None),
            P("wide", None),
            P(),
            P(None, "wide"),
            P(),
            P("wide"),
            P(),
            P("wide"),
            P(),
            P("wide"),
            P(),
            P(),
            P(None, "wide", None),
            P("wide", None),
            P("wide", None),
            P("wide", None),
            P(),
        ),
        check_vma=False,
    )
```

profile of v0, /device:TPU:0, one launch (start us, length us, event | category | flops | bytes accessed | tf_op | source)
XLA Modules:
  0.0 361.8 jit_solution(14774326667067611419)
XLA Ops:
  1.3 3.8 %pick.1 = (bf16[2,48,768]{2,1,0:T(8,128)(2,1)}, bf16[1,48,768]{2,1,0:T(8,128)(2,1)}, bf16[528,256]{1,0:T(8,128)(2,1)}, bf16[768,256]{1,0:T(8,128)(2,1)}) custom-call(s32[4]{0:T(128)} %pad_add_fusion.place, f32[3,96,768]{2,1,0:T(8,128)} %inward.1, f32[96,768]{1,0:T(8,128)} %out.1, f32[96,3072]{1,0:T(8,128)} %up.1, f32[384,768]{1,0:T(8,128)} %down.1), custom_call_target="tpu_custom_call" | custom-call | flops 1000000 | bytes 100000 | tf_op jit(solution)/shard_map/pick/pallas_call | solution.py:1015
  5.1 4.0 %collective-permute-start.4 = (bf16[1,48,768]{2,1,0:T(8,128)(2,1)}, bf16[1,48,768]{2,1,0:T(8,128)(2,1)S(1)}, u32[]{:S(2)}, u32[]{:S(2)}) collective-permute-start(bf16[1,48,768]{2,1,0:T(8,128)(2,1)} %get-tuple-element.176), channel_id=1, source_target_pairs={{0,16},{4,20},{8,24},{12,28},{16,0},{20,4},{24,8},{28,12},{1,17},{... | collective-permute-start | bytes 221192 | tf_op jit(solution)/shard_map/ppermute | solution.py:968
  16.2 3.1 multiply_sine_fusion
  21.1 5.1 %collective-permute-done.1 = bf16[2,48,768]{2,1,0:T(8,128)(2,1)S(1)} collective-permute-done((bf16[2,48,768]{2,1,0:T(8,128)(2,1)}, bf16[2,48,768]{2,1,0:T(8,128)(2,1)S(1)}, u32[]{:S(2)}, u32[]{:S(2)}) %collective-permute-start.1) | collective-permute-done | bytes 147488 | tf_op jit(solution)/shard_map/ppermute | solution.py:968
  31.5 3.2 collective-permute-start.9
  35.3 6.4 %collective-permute-done.8 = bf16[528,256]{1,0:T(8,128)(2,1)S(1)} collective-permute-done((bf16[528,256]{1,0:T(8,128)(2,1)S(1)}, bf16[528,256]{1,0:T(8,128)(2,1)S(1)}, u32[]{:S(2)}, u32[]{:S(2)}) %collective-permute-start.8) | collective-permute-done | bytes 270368 | tf_op jit(solution)/shard_map/ppermute | solution.py:968
  41.6 10.4 %collective-permute-done.9 = bf16[528,256]{1,0:T(8,128)(2,1)S(1)} collective-permute-done((bf16[528,256]{1,0:T(8,128)(2,1)S(1)}, bf16[528,256]{1,0:T(8,128)(2,1)S(1)}, u32[]{:S(2)}, u32[]{:S(2)}) %collective-permute-start.9) | collective-permute-done | bytes 270368 | tf_op jit(solution)/shard_map/ppermute | solution.py:968
  57.5 6.3 %collective-permute-start.17 = (bf16[768,256]{1,0:T(8,128)(2,1)}, bf16[768,256]{1,0:T(8,128)(2,1)}, u32[]{:S(2)}, u32[]{:S(2)}) collective-permute-start(bf16[768,256]{1,0:T(8,128)(2,1)} %get-tuple-element.201), channel_id=1, source_target_pairs={{0,8},{4,12},{8,16},{12,20},{16,24},{20,28},{24,0},{28,4},{1,9},{5... | collective-permute-start | bytes 1179656 | tf_op jit(solution)/shard_map/ppermute | solution.py:968
  67.6 33.2 %attend.1 = (bf16[1024,768]{1,0:T(8,128)(2,1)}, f32[3,1024,256]{2,1,0:T(8,128)}, bf16[768,1024]{1,0:T(8,128)(2,1)}, bf16[8,288,768]{2,1,0:T(8,128)(2,1)}, f32[3,...) custom-call(s32[1,24]{1,0:T(1,128)} %lengths.3, ...), custom_call_target="tpu_custom_call" | custom-call | flops 1000000 | bytes 100000 | tf_op jit(solution)/shard_map/attend/pallas_call | solution.py:317
  107.2 28.6 %middle_first.1 = (f32[1024,768]{1,0:T(8,128)}, bf16[1024,768]{1,0:T(8,128)(2,1)}, bf16[768,1024]{1,0:T(8,128)(2,1)}, bf16[768,1024]{1,0:T(8,128)(2,1)}, f32[102...) custom-call(s32[4]{0:T(128)} %pad_add_fusion.place, ...), custom_call_target="tpu_custom_call" | custom-call | flops 1000000 | bytes 100000 | tf_op jit(solution)/shard_map/middle_first/pallas_call | solution.py:793
  135.9 5.9 %collective-permute-done.21.refs_1_ = bf16[4,768,256]{2,1,0:T(8,128)(2,1)} collective-permute-done((bf16[4,768,256]{2,1,0:T(8,128)(2,1)S(1)}, bf16[4,768,256]{2,1,0:T(8,128)(2,1)}, u32[]{:S(2)}, u32[]{:S(2)}) %collective-permute-start.21) | collective-permute-done | bytes 1572896 | tf_op jit(solution)/shard_map/ppermute | solution.py:972
  143.4 3.1 collective-permute-done.23.refs_3_
  147.7 47.8 %middle_rest.1 = (f32[1024,768]{1,0:T(8,128)}, f32[1024,768]{1,0:T(8,128)}, f32[1024,768]{1,0:T(8,128)}, bf16[8,144,256]{2,1,0:T(8,128)(2,1)S(1)}, bf16[8,144,25...) custom-call(s32[4]{0:T(128)} %pad_add_fusion.place, ...), custom_call_target="tpu_custom_call" | custom-call | flops 1000000 | bytes 100000 | tf_op jit(solution)/shard_map/middle_rest/pallas_call | solution.py:832
  196.2 6.0 %collective-permute-done.26.refs_3_ = bf16[8,144,256]{2,1,0:T(8,128)(2,1)S(1)} collective-permute-done((bf16[8,144,256]{2,1,0:T(8,128)(2,1)S(1)}, bf16[8,144,256]{2,1,0:T(8,128)(2,1)S(1)}, u32[]{:S(2)}, u32[]{:S(2)}) %collective-permute-start.26) | collective-permute-done | bytes 589856 | tf_op jit(solution)/shard_map/ppermute | solution.py:984
  210.4 44.6 %attend_back.1 = (bf16[3,8,144,256]{3,2,1,0:T(8,128)(2,1)S(1)}, bf16[3,8,144,256]{3,2,1,0:T(8,128)(2,1)S(1)}, f32[3,1,768]{2,1,0:T(1,128)S(1)}, f32[1024,768]{1,0:T(8,128)}) custom-call(s32[1,24]{1,0:T(1,128)S(1)} %copy-done.12, s32[4]{0:T(128)S(1)} %copy-done.7, f32[1024,768]{1,0:T(8,128)} %get-tuple-element.238.dmixed_ref, ...), custom_call_target="tpu_custom_call" | custom-call | flops 1000000 | bytes 100000 | tf_op jit(solution)/shard_map/attend_back/pallas_call | solution.py:504
  258.2 3.7 %collective-permute-done.31.got = bf16[3,8,144,256]{3,2,1,0:T(8,128)(2,1)S(1)} collective-permute-done((bf16[3,8,144,256]{3,2,1,0:T(8,128)(2,1)S(1)}, bf16[3,8,144,256]{3,2,1,0:T(8,128)(2,1)S(1)}, u32[]{:S(2)}, u32[]{:S(2)}) %collective-permute-start.31) | collective-permute-done | bytes 1769504 | tf_op jit(solution)/shard_map/ppermute | solution.py:984
  263.0 5.0 %collective-permute-start.32 = (bf16[8,432,128]{2,1,0:T(8,128)(2,1)S(1)}, bf16[8,432,128]{2,1,0:T(8,128)(2,1)S(1)}, u32[]{:S(2)}, u32[]{:S(2)}) collective-permute-start(bf16[8,432,128]{2,1,0:T(8,128)(2,1)S(1)} %get-tuple-element.266), channel_id=1, source_target_pairs={{0,2},{1,3},{2,0},{3,1},{4,6},{5,7},{6,4},{7,5},{8,10},{9,11},{10,... | collective-permute-start | bytes 2654216 | tf_op jit(solution)/shard_map/ppermute | solution.py:980
  268.0 3.1 collective-permute-start.34
  271.1 2.9 collective-permute-start.35
  274.0 6.4 %input_side.1 = (f32[1024,768]{1,0:T(8,128)}, f32[16,768]{1,0:T(8,128)}) custom-call(bf16[1024,768]{1,0:T(8,128)(2,1)} %x_ref.1, f32[1024,768]{1,0:T(8,128)} %get-tuple-element.267.dx1_ref, f32[1024,768]{1,0:T(8,128)} %get-tuple-element.268.da1_ref, f32[13,768]{1,0:T(8,128)} %vectors.1, f32[8,768]{1,0:T(8,128)} %get-tuple-element.269.middle_ref, ...), custom_call_target="tpu_custom_call" | custom-call | flops 1000000 | bytes 100000 | tf_op jit(solution)/shard_map/input_side/pallas_call | solution.py:904
  280.4 7.8 %collective-permute-done.32.got = bf16[8,432,128]{2,1,0:T(8,128)(2,1)S(1)} collective-permute-done((bf16[8,432,128]{2,1,0:T(8,128)(2,1)S(1)}, bf16[8,432,128]{2,1,0:T(8,128)(2,1)S(1)}, u32[]{:S(2)}, u32[]{:S(2)}) %collective-permute-start.32) | collective-permute-done | bytes 884768 | tf_op jit(solution)/shard_map/ppermute | solution.py:980
  289.0 9.2 %collective-permute-done.34.refs_2_ = bf16[768,256]{1,0:T(8,128)(2,1)} collective-permute-done((bf16[768,256]{1,0:T(8,128)(2,1)}, bf16[768,256]{1,0:T(8,128)(2,1)}, u32[]{:S(2)}, u32[]{:S(2)}) %collective-permute-start.34) | collective-permute-done | bytes 393248 | tf_op jit(solution)/shard_map/ppermute | solution.py:968
  303.2 5.9 %collective-permute-start.39 = (bf16[432,128]{1,0:T(8,128)(2,1)S(1)}, bf16[432,128]{1,0:T(8,128)(2,1)S(1)}, u32[]{:S(2)}, u32[]{:S(2)}) collective-permute-start(bf16[432,128]{1,0:T(8,128)(2,1)S(1)} %get-tuple-element.296), channel_id=1, source_target_pairs={{0,8},{4,12},{8,16},{12,20},{16,24},{20,28},{24,0},{28,4},{1,9},{5... | collective-permute-start | bytes 331784 | tf_op jit(solution)/shard_map/ppermute | solution.py:968
  309.1 2.5 collective-permute-start.40
  311.8 3.3 collective-permute-done.39.refs_1_
  315.2 3.1 collective-permute-done.40.refs_2_
  321.6 6.8 %collective-permute-done.43 = f32[16,768]{1,0:T(8,128)S(1)} collective-permute-done((f32[16,768]{1,0:T(8,128)S(1)}, f32[16,768]{1,0:T(8,128)S(1)}, u32[]{:S(2)}, u32[]{:S(2)}) %collective-permute-start.43) | collective-permute-done | bytes 49184 | tf_op jit(solution)/shard_map/ppermute | solution.py:980
  328.5 3.0 ffn_moments.1
  334.9 5.2 %collective-permute-done.48 = f32[40,768]{1,0:T(8,128)S(1)} collective-permute-done((f32[40,768]{1,0:T(8,128)S(1)}, f32[40,768]{1,0:T(8,128)S(1)}, u32[]{:S(2)}, u32[]{:S(2)}) %collective-permute-start.48) | collective-permute-done | bytes 122912 | tf_op jit(solution)/shard_map/ppermute | solution.py:999
  340.1 5.6 %collective-permute-start.49 = (f32[40,768]{1,0:T(8,128)S(1)}, f32[40,768]{1,0:T(8,128)S(1)}, u32[]{:S(2)}, u32[]{:S(2)}) collective-permute-start(f32[40,768]{1,0:T(8,128)S(1)} %add.28), channel_id=1, source_target_pairs={{0,8},{4,12},{8,0},{12,4},{16,24},{20,28},{24,16},{28,20},{1,9},{5... | collective-permute-start | bytes 368648 | tf_op jit(solution)/shard_map/ppermute | solution.py:999
  345.7 2.9 collective-permute-done.49
  355.3 6.2 %finish.1 = (f32[3,768]{1,0:T(4,128)}, f32[3072]{0:T(1024)}, f32[768]{0:T(1024)}, f32[768]{0:T(1024)}, f32[3,96,768]{2,1,0:T(8,128)}, /*index=5*/f32[96,3072]{1,...) custom-call(s32[4]{0:T(128)} %pad_add_fusion.place, ...), custom_call_target="tpu_custom_call" | custom-call | flops 1000000 | bytes 100000 | tf_op jit(solution)/shard_map/finish/pallas_call | solution.py:1015
  (213 shorter events, 66.1 us)
Async XLA Ops:
  5.1 14.9 %collective-permute-start.4 = (bf16[1,48,768]{2,1,0:T(8,128)(2,1)}, bf16[1,48,768]{2,1,0:T(8,128)(2,1)S(1)}, u32[]{:S(2)}, u32[]{:S(2)}) collective-permute-start(bf16[1,48,768]{2,1,0:T(8,128)(2,1)} %get-tuple-element.176), channel_id=1, source_target_pairs={{0,16},{4,20},{8,24},{12,28},{16,0},{20,4},{24,8},{28,12},{1,17},{... | collective-permute-start | bytes 221192 | tf_op jit(solution)/shard_map/ppermute | solution.py:968
  9.1 11.9 %collective-permute-start.5 = (bf16[1,48,768]{2,1,0:T(8,128)(2,1)}, bf16[1,48,768]{2,1,0:T(8,128)(2,1)S(1)}, u32[]{:S(2)}, u32[]{:S(2)}) collective-permute-start(bf16[1,48,768]{2,1,0:T(8,128)(2,1)} %get-tuple-element.176), channel_id=1, source_target_pairs={{0,24},{4,28},{8,0},{12,4},{16,8},{20,12},{24,16},{28,20},{1,25},{... | collective-permute-start | bytes 221192 | tf_op jit(solution)/shard_map/ppermute | solution.py:968
  10.5 10.6 %collective-permute-start.3 = (bf16[1,48,768]{2,1,0:T(8,128)(2,1)}, bf16[1,48,768]{2,1,0:T(8,128)(2,1)S(1)}, u32[]{:S(2)}, u32[]{:S(2)}) collective-permute-start(bf16[1,48,768]{2,1,0:T(8,128)(2,1)} %get-tuple-element.176), channel_id=1, source_target_pairs={{0,8},{4,12},{8,16},{12,20},{16,24},{20,28},{24,0},{28,4},{1,9},{5... | collective-permute-start | bytes 221192 | tf_op jit(solution)/shard_map/ppermute | solution.py:968
  11.1 10.0 %collective-permute-start = (bf16[2,48,768]{2,1,0:T(8,128)(2,1)}, bf16[2,48,768]{2,1,0:T(8,128)(2,1)S(1)}, u32[]{:S(2)}, u32[]{:S(2)}) collective-permute-start(bf16[2,48,768]{2,1,0:T(8,128)(2,1)} %get-tuple-element.175), channel_id=1, source_target_pairs={{0,8},{4,12},{8,16},{12,20},{16,24},{20,28},{24,0},{28,4},{1,9},{5... | collective-permute-start | bytes 442376 | tf_op jit(solution)/shard_map/ppermute | solution.py:968
  12.7 13.6 %collective-permute-start.1 = (bf16[2,48,768]{2,1,0:T(8,128)(2,1)}, bf16[2,48,768]{2,1,0:T(8,128)(2,1)S(1)}, u32[]{:S(2)}, u32[]{:S(2)}) collective-permute-start(bf16[2,48,768]{2,1,0:T(8,128)(2,1)} %get-tuple-element.175), channel_id=1, source_target_pairs={{0,16},{4,20},{8,24},{12,28},{16,0},{20,4},{24,8},{28,12},{1,17},{... | collective-permute-start | bytes 442376 | tf_op jit(solution)/shard_map/ppermute | solution.py:968
  27.5 24.7 %collective-permute-start.6 = (bf16[4,2,48,768]{3,2,1,0:T(8,128)(2,1)S(1)}, bf16[4,2,48,768]{3,2,1,0:T(8,128)(2,1)S(1)}, u32[]{:S(2)}, u32[]{:S(2)}) collective-permute-start(bf16[4,2,48,768]{3,2,1,0:T(8,128)(2,1)S(1)} %pad_maximum_fusion.2.refs_0_), channel_id=1, source_target_pairs={{0,4},{4,0},{8,12},{12,8},{16,20},{20,16},{24,28},{28,24},{1,5},{5... | collective-permute-start | bytes 1769480 | tf_op jit(solution)/shard_map/ppermute | solution.py:972
  29.3 12.3 %collective-permute-start.8 = (bf16[528,256]{1,0:T(8,128)(2,1)S(1)}, bf16[528,256]{1,0:T(8,128)(2,1)S(1)}, u32[]{:S(2)}, u32[]{:S(2)}) collective-permute-start(bf16[528,256]{1,0:T(8,128)(2,1)S(1)} %copy-done.32), channel_id=1, source_target_pairs={{0,8},{4,12},{8,16},{12,20},{16,24},{20,28},{24,0},{28,4},{1,9},{5... | collective-permute-start | bytes 811016 | tf_op jit(solution)/shard_map/ppermute | solution.py:968
  31.5 20.6 %collective-permute-start.9 = (bf16[528,256]{1,0:T(8,128)(2,1)S(1)}, bf16[528,256]{1,0:T(8,128)(2,1)S(1)}, u32[]{:S(2)}, u32[]{:S(2)}) collective-permute-start(bf16[528,256]{1,0:T(8,128)(2,1)S(1)} %copy-done.32), channel_id=1, source_target_pairs={{0,16},{4,20},{8,24},{12,28},{16,0},{20,4},{24,8},{28,12},{1,17},{... | collective-permute-start | bytes 811016 | tf_op jit(solution)/shard_map/ppermute | solution.py:968
  34.7 17.4 %collective-permute-start.10 = (bf16[528,256]{1,0:T(8,128)(2,1)S(1)}, bf16[528,256]{1,0:T(8,128)(2,1)S(1)}, u32[]{:S(2)}, u32[]{:S(2)}) collective-permute-start(bf16[528,256]{1,0:T(8,128)(2,1)S(1)} %copy-done.32), channel_id=1, source_target_pairs={{0,24},{4,28},{8,0},{12,4},{16,8},{20,12},{24,16},{28,20},{1,25},{... | collective-permute-start | bytes 811016 | tf_op jit(solution)/shard_map/ppermute | solution.py:968
  34.7 17.5 %collective-permute-start.7 = (bf16[4,1,48,768]{3,2,1,0:T(8,128)(2,1)S(1)}, bf16[4,1,48,768]{3,2,1,0:T(8,128)(2,1)S(1)}, u32[]{:S(2)}, u32[]{:S(2)}) collective-permute-start(bf16[4,1,48,768]{3,2,1,0:T(8,128)(2,1)S(1)} %pad_maximum_fusion.4.refs_4_), channel_id=1, source_target_pairs={{0,4},{4,0},{8,12},{12,8},{16,20},{20,16},{24,28},{28,24},{1,5},{5... | collective-permute-start | bytes 884744 | tf_op jit(solution)/shard_map/ppermute | solution.py:972
  57.0 43.9 %collective-permute-start.16 = (bf16[4,528,256]{2,1,0:T(8,128)(2,1)S(1)}, bf16[4,528,256]{2,1,0:T(8,128)(2,1)}, u32[]{:S(2)}, u32[]{:S(2)}) collective-permute-start(bf16[4,528,256]{2,1,0:T(8,128)(2,1)S(1)} %pad_maximum_fusion.1.refs_0_), channel_id=1, source_target_pairs={{0,4},{4,0},{8,12},{12,8},{16,20},{20,16},{24,28},{28,24},{1,5},{5... | collective-permute-start | bytes 3244040 | tf_op jit(solution)/shard_map/ppermute | solution.py:972
  57.5 43.4 %collective-permute-start.17 = (bf16[768,256]{1,0:T(8,128)(2,1)}, bf16[768,256]{1,0:T(8,128)(2,1)}, u32[]{:S(2)}, u32[]{:S(2)}) collective-permute-start(bf16[768,256]{1,0:T(8,128)(2,1)} %get-tuple-element.201), channel_id=1, source_target_pairs={{0,8},{4,12},{8,16},{12,20},{16,24},{20,28},{24,0},{28,4},{1,9},{5... | collective-permute-start | bytes 1179656 | tf_op jit(solution)/shard_map/ppermute | solution.py:968
  63.8 37.1 %collective-permute-start.18 = (bf16[768,256]{1,0:T(8,128)(2,1)}, bf16[768,256]{1,0:T(8,128)(2,1)}, u32[]{:S(2)}, u32[]{:S(2)}) collective-permute-start(bf16[768,256]{1,0:T(8,128)(2,1)} %get-tuple-element.201), channel_id=1, source_target_pairs={{0,16},{4,20},{8,24},{12,28},{16,0},{20,4},{24,8},{28,12},{1,17},{... | collective-permute-start | bytes 1179656 | tf_op jit(solution)/shard_map/ppermute | solution.py:968
  63.8 37.1 %collective-permute-start.19 = (bf16[768,256]{1,0:T(8,128)(2,1)}, bf16[768,256]{1,0:T(8,128)(2,1)}, u32[]{:S(2)}, u32[]{:S(2)}) collective-permute-start(bf16[768,256]{1,0:T(8,128)(2,1)} %get-tuple-element.201), channel_id=1, source_target_pairs={{0,24},{4,28},{8,0},{12,4},{16,8},{20,12},{24,16},{28,20},{1,25},{... | collective-permute-start | bytes 1179656 | tf_op jit(solution)/shard_map/ppermute | solution.py:968
  67.6 35.4 %collective-permute-start.15 = (bf16[4,528,256]{2,1,0:T(8,128)(2,1)S(1)}, bf16[4,528,256]{2,1,0:T(8,128)(2,1)}, u32[]{:S(2)}, u32[]{:S(2)}) collective-permute-start(bf16[4,528,256]{2,1,0:T(8,128)(2,1)S(1)} %pad_maximum_fusion.1.refs_0_), channel_id=1, source_target_pairs={{0,1},{1,0},{2,3},{3,2},{4,5},{5,4},{6,7},{7,6},{8,9},{9,8},{10,11... | collective-permute-start | bytes 3244040 | tf_op jit(solution)/shard_map/ppermute | solution.py:984
  105.0 36.8 %collective-permute-start.21 = (bf16[4,768,256]{2,1,0:T(8,128)(2,1)S(1)}, bf16[4,768,256]{2,1,0:T(8,128)(2,1)}, u32[]{:S(2)}, u32[]{:S(2)}) collective-permute-start(bf16[4,768,256]{2,1,0:T(8,128)(2,1)S(1)} %pad_maximum_fusion.refs_0_), channel_id=1, source_target_pairs={{0,4},{4,0},{8,12},{12,8},{16,20},{20,16},{24,28},{28,24},{1,5},{5... | collective-permute-start | bytes 4718600 | tf_op jit(solution)/shard_map/ppermute | solution.py:972
  106.5 35.3 %collective-permute-start.22 = (bf16[4,768,256]{2,1,0:T(8,128)(2,1)S(1)}, bf16[4,768,256]{2,1,0:T(8,128)(2,1)S(1)}, u32[]{:S(2)}, u32[]{:S(2)}) collective-permute-start(bf16[4,768,256]{2,1,0:T(8,128)(2,1)S(1)} %pad_maximum_fusion.refs_0_), channel_id=1, source_target_pairs={{0,1},{1,0},{2,3},{3,2},{4,5},{5,4},{6,7},{7,6},{8,9},{9,8},{10,11... | collective-permute-start | bytes 4718600 | tf_op jit(solution)/shard_map/ppermute | solution.py:984
  142.9 52.6 %collective-permute-start.24 = (bf16[8,384,256]{2,1,0:T(8,128)(2,1)}, bf16[8,384,256]{2,1,0:T(8,128)(2,1)S(1)}, u32[]{:S(2)}, u32[]{:S(2)}) collective-permute-start(bf16[8,384,256]{2,1,0:T(8,128)(2,1)} %get-tuple-element.224), channel_id=1, source_target_pairs={{0,1},{1,0},{2,3},{3,2},{4,5},{5,4},{6,7},{7,6},{8,9},{9,8},{10,11... | collective-permute-start | bytes 4718600 | tf_op jit(solution)/shard_map/ppermute | solution.py:984
  204.9 50.0 %collective-permute-start.30 = (bf16[4,768,256]{2,1,0:T(8,128)(2,1)S(1)}, bf16[4,768,256]{2,1,0:T(8,128)(2,1)S(1)}, u32[]{:S(2)}, u32[]{:S(2)}) collective-permute-start(bf16[4,768,256]{2,1,0:T(8,128)(2,1)S(1)} %get-tuple-element.254), channel_id=1, source_target_pairs={{0,4},{4,0},{8,12},{12,8},{16,20},{20,16},{24,28},{28,24},{1,5},{5... | collective-permute-start | bytes 4718600 | tf_op jit(solution)/shard_map/ppermute | solution.py:972
  206.5 50.2 %collective-permute-start.27 = (bf16[2,528,256]{2,1,0:T(8,128)(2,1)S(1)}, bf16[2,528,256]{2,1,0:T(8,128)(2,1)S(1)}, u32[]{:S(2)}, u32[]{:S(2)}) collective-permute-start(bf16[2,528,256]{2,1,0:T(8,128)(2,1)S(1)} %get-tuple-element.250), channel_id=1, source_target_pairs={{0,8},{4,12},{8,16},{12,20},{16,24},{20,28},{24,0},{28,4},{1,9},{5... | collective-permute-start | bytes 1622024 | tf_op jit(solution)/shard_map/ppermute | solution.py:968
  207.7 49.0 %collective-permute-start.28 = (bf16[2,528,256]{2,1,0:T(8,128)(2,1)S(1)}, bf16[2,528,256]{2,1,0:T(8,128)(2,1)S(1)}, u32[]{:S(2)}, u32[]{:S(2)}) collective-permute-start(bf16[2,528,256]{2,1,0:T(8,128)(2,1)S(1)} %get-tuple-element.251), channel_id=1, source_target_pairs={{0,16},{4,20},{8,24},{12,28},{16,0},{20,4},{24,8},{28,12},{1,17},{... | collective-permute-start | bytes 1622024 | tf_op jit(solution)/shard_map/ppermute | solution.py:968
  209.8 46.9 %collective-permute-start.29 = (bf16[2,528,256]{2,1,0:T(8,128)(2,1)S(1)}, bf16[2,528,256]{2,1,0:T(8,128)(2,1)S(1)}, u32[]{:S(2)}, u32[]{:S(2)}) collective-permute-start(bf16[2,528,256]{2,1,0:T(8,128)(2,1)S(1)} %get-tuple-element.252), channel_id=1, source_target_pairs={{0,24},{4,28},{8,0},{12,4},{16,8},{20,12},{24,16},{28,20},{1,25},{... | collective-permute-start | bytes 1622024 | tf_op jit(solution)/shard_map/ppermute | solution.py:968
  263.0 25.1 %collective-permute-start.32 = (bf16[8,432,128]{2,1,0:T(8,128)(2,1)S(1)}, bf16[8,432,128]{2,1,0:T(8,128)(2,1)S(1)}, u32[]{:S(2)}, u32[]{:S(2)}) collective-permute-start(bf16[8,432,128]{2,1,0:T(8,128)(2,1)S(1)} %get-tuple-element.266), channel_id=1, source_target_pairs={{0,2},{1,3},{2,0},{3,1},{4,6},{5,7},{6,4},{7,5},{8,10},{9,11},{10,... | collective-permute-start | bytes 2654216 | tf_op jit(solution)/shard_map/ppermute | solution.py:980
  268.0 21.0 %collective-permute-start.33 = (bf16[768,256]{1,0:T(8,128)(2,1)}, bf16[768,256]{1,0:T(8,128)(2,1)S(1)}, u32[]{:S(2)}, u32[]{:S(2)}) collective-permute-start(bf16[768,256]{1,0:T(8,128)(2,1)} %get-tuple-element.281), channel_id=1, source_target_pairs={{0,8},{4,12},{8,16},{12,20},{16,24},{20,28},{24,0},{28,4},{1,9},{5... | collective-permute-start | bytes 1179656 | tf_op jit(solution)/shard_map/ppermute | solution.py:968
  268.0 30.2 %collective-permute-start.34 = (bf16[768,256]{1,0:T(8,128)(2,1)}, bf16[768,256]{1,0:T(8,128)(2,1)}, u32[]{:S(2)}, u32[]{:S(2)}) collective-permute-start(bf16[768,256]{1,0:T(8,128)(2,1)} %get-tuple-element.282), channel_id=1, source_target_pairs={{0,16},{4,20},{8,24},{12,28},{16,0},{20,4},{24,8},{28,12},{1,17},{... | collective-permute-start | bytes 1179656 | tf_op jit(solution)/shard_map/ppermute | solution.py:968
  271.1 27.1 %collective-permute-start.35 = (bf16[768,256]{1,0:T(8,128)(2,1)}, bf16[768,256]{1,0:T(8,128)(2,1)}, u32[]{:S(2)}, u32[]{:S(2)}) collective-permute-start(bf16[768,256]{1,0:T(8,128)(2,1)} %get-tuple-element.283), channel_id=1, source_target_pairs={{0,24},{4,28},{8,0},{12,4},{16,8},{20,12},{24,16},{28,20},{1,25},{... | collective-permute-start | bytes 1179656 | tf_op jit(solution)/shard_map/ppermute | solution.py:968
  274.0 15.0 %collective-permute-start.36 = (bf16[528,256]{1,0:T(8,128)(2,1)}, bf16[528,256]{1,0:T(8,128)(2,1)}, u32[]{:S(2)}, u32[]{:S(2)}) collective-permute-start(bf16[528,256]{1,0:T(8,128)(2,1)} %get-tuple-element.285), channel_id=1, source_target_pairs={{0,4},{4,0},{8,12},{12,8},{16,20},{20,16},{24,28},{28,24},{1,5},{5... | collective-permute-start | bytes 811016 | tf_op jit(solution)/shard_map/ppermute | solution.py:972
  288.9 12.0 %collective-permute-start.37 = (bf16[4,432,128]{2,1,0:T(8,128)(2,1)S(1)}, bf16[4,432,128]{2,1,0:T(8,128)(2,1)S(1)}, u32[]{:S(2)}, u32[]{:S(2)}) collective-permute-start(bf16[4,432,128]{2,1,0:T(8,128)(2,1)S(1)} %get-tuple-element.286), channel_id=1, source_target_pairs={{0,4},{4,0},{8,12},{12,8},{16,20},{20,16},{24,28},{28,24},{1,5},{5... | collective-permute-start | bytes 1327112 | tf_op jit(solution)/shard_map/ppermute | solution.py:972
  301.7 17.6 %collective-permute-start.38 = (bf16[1296,256]{1,0:T(8,128)(2,1)S(1)}, bf16[1296,256]{1,0:T(8,128)(2,1)S(1)}, u32[]{:S(2)}, u32[]{:S(2)}) collective-permute-start(bf16[1296,256]{1,0:T(8,128)(2,1)S(1)} %z_sum.2), channel_id=1, source_target_pairs={{0,2},{1,3},{2,0},{3,1},{4,6},{5,7},{6,4},{7,5},{8,10},{9,11},{10,... | collective-permute-start | bytes 1990664 | tf_op jit(solution)/shard_map/ppermute | solution.py:980
  303.2 11.9 %collective-permute-start.39 = (bf16[432,128]{1,0:T(8,128)(2,1)S(1)}, bf16[432,128]{1,0:T(8,128)(2,1)S(1)}, u32[]{:S(2)}, u32[]{:S(2)}) collective-permute-start(bf16[432,128]{1,0:T(8,128)(2,1)S(1)} %get-tuple-element.296), channel_id=1, source_target_pairs={{0,8},{4,12},{8,16},{12,20},{16,24},{20,28},{24,0},{28,4},{1,9},{5... | collective-permute-start | bytes 331784 | tf_op jit(solution)/shard_map/ppermute | solution.py:968
  309.1 9.1 %collective-permute-start.40 = (bf16[432,128]{1,0:T(8,128)(2,1)S(1)}, bf16[432,128]{1,0:T(8,128)(2,1)S(1)}, u32[]{:S(2)}, u32[]{:S(2)}) collective-permute-start(bf16[432,128]{1,0:T(8,128)(2,1)S(1)} %get-tuple-element.297), channel_id=1, source_target_pairs={{0,16},{4,20},{8,24},{12,28},{16,0},{20,4},{24,8},{28,12},{1,17},{... | collective-permute-start | bytes 331784 | tf_op jit(solution)/shard_map/ppermute | solution.py:968
  321.6 10.4 %collective-permute-start.45 = (f32[432,128]{1,0:T(8,128)S(1)}, f32[432,128]{1,0:T(8,128)S(1)}, u32[]{:S(2)}, u32[]{:S(2)}) collective-permute-start(f32[432,128]{1,0:T(8,128)S(1)} %z_sum.3.own), channel_id=1, source_target_pairs={{0,1},{1,0},{2,3},{3,2},{4,5},{5,4},{6,7},{7,6},{8,9},{9,8},{10,11... | collective-permute-start | bytes 663560 | tf_op jit(solution)/shard_map/ppermute | solution.py:984
  (61 other events, 707.2 us)
where the time goes:
time: 368 us; the launch traced here: 362 us
  Pallas kernels  185 us (50%)
  waiting for transfers between devices  88.3 us (24%)
  starting transfers between devices  68.8 us (19%)
  other arithmetic  9.8 us (3%)
  local copies, waits for them, and re-layouts  7.84 us (2%)
    pallas_call x1, Pallas kernels, middle_rest(): pl.pallas_call(functools.partial(middle_rest_kernel, wide, len(pieces)),...  47.8 us
    pallas_call x1, Pallas kernels, attend_back(): pl.pallas_call(attend_back_kernel, grid_spec=pltpu.PrefetchScalarGridSpec...  44.6 us
    ppermute x21, starting transfers between devices, over_z(): return lax.ppermute(values, 'wide', wide_perm(shift, False))  42.5 us
    ppermute x21, waiting for transfers between devices, over_z(): return lax.ppermute(values, 'wide', wide_perm(shift, False))  39.1 us
    pallas_call x1, Pallas kernels, attend(): pl.pallas_call(functools.partial(attend_kernel, len(pieces)), grid_spec=p...  33.2 us
    pallas_call x1, Pallas kernels, middle_first(): pl.pallas_call(functools.partial(middle_first_kernel, wide, len(pieces)),...  28.6 us
    ppermute x16, waiting for transfers between devices, over_core(): return lax.ppermute(values, 'narrow', narrow_perm(False, True))  17.5 us
    pallas_call x11, Pallas kernels, held_call(): pl.pallas_call(kernel, in_specs=[pl.BlockSpec(memory_space=pltpu.SMEM)] +...  14.7 us
  transfers between devices with their start and end apart: 51, of which 22 were waited for; matrix products, arithmetic and copies ran while one was open for 3% of the time, Pallas kernels for 47%

commit v1 on v0

--- a/solution.py
+++ b/solution.py
@@ -1497,12 +1497,12 @@
         lengths, place, wide, dmixed, saved, a1t, w_in, perm, proj, cosine, sine, onehot, ones
     )
     if full:
+        in_send, da1, got_b, *e_got = tie(in_send, da1, got_b, *e_got)
         b_parts = list(second_sum(place, keep_b, got_b))
-        in_send, da1, *e_got, b_parts[1] = tie(in_send, da1, *e_got, b_parts[1])
+        got_in = over_core(in_send)
+        got_in, *e_got, b_parts[1] = tie(got_in, *e_got, b_parts[1])
         keep_e, send_e = split_sum(place, [e_parts[0]] + e_got)
-        send_e, in_send = tie(send_e, in_send)
         got_e = over_x(send_e)
-        got_in = over_core(in_send)
         send_c, keep_c = held_call(
             first_sum_y_kernel, "first_sum_y", place, [in_keep, got_in],
             [struct((8, 432, 128), BF16)] * 2,
@@ -1531,8 +1531,7 @@
         c_mine = z_sum(place, c_parts)
         c_mine, vector_local = tie(c_mine, vector_local)
         c_y = over_y(c_mine)
-        c_y, vector_y = tie(c_y, over_y(vector_local))
-        vector_pair = vector_local + vector_y
+        vector_y = over_y(vector_local)
         c_core = over_core(c_mine)
         ffn_y, c_mine = tie(ffn_y, c_mine)
         ffn_own, ffn_got = pair_sum(ffn_mine, ffn_y)
@@ -1548,7 +1547,8 @@
             ],
             0,
         )
-        c_y, sums = tie(c_y, sums)
+        c_y, vector_y, sums = tie(c_y, vector_y, sums)
+        vector_pair = vector_local + vector_y
         inward_grad, in_rows, sums = held_call(
             in_moments_kernel, "in_moments", place,
             [

time: 368 us -> 363 us (0.986)
  waiting for transfers between devices: 88.3 us -> 78.9 us
  starting transfers between devices: 68.8 us -> 72.7 us
    ppermute x21, waiting for transfers between devices: 39.1 us -> 33.2 us  [over_z(): return lax.ppermute(values, 'wide', wide_perm(shift, False))]
    ppermute x7, starting transfers between devices: 5.98 us -> 10.9 us  [over_x(): return lax.ppermute(values, 'wide', wide_perm(0, True))]
    ppermute x4, waiting for transfers between devices: 14.6 us -> 9.81 us  [over_y(): return lax.ppermute(values, 'narrow', narrow_perm(True, False))]
where the time goes in v1:
time: 363 us; the launch traced here: 358 us
  Pallas kernels  186 us (51%)
  waiting for transfers between devices  78.9 us (22%)
  starting transfers between devices  72.7 us (20%)
  other arithmetic  9.8 us (3%)
  local copies, waits for them, and re-layouts  8.54 us (2%)
    pallas_call x1, Pallas kernels, middle_rest(): pl.pallas_call(functools.partial(middle_rest_kernel, wide, len(pieces)),...  47.8 us
    pallas_call x1, Pallas kernels, attend_back(): pl.pallas_call(attend_back_kernel, grid_spec=pltpu.PrefetchScalarGridSpec...  44.6 us
    ppermute x21, starting transfers between devices, over_z(): return lax.ppermute(values, 'wide', wide_perm(shift, False))  41.2 us
    ppermute x21, waiting for transfers between devices, over_z(): return lax.ppermute(values, 'wide', wide_perm(shift, False))  33.2 us
    pallas_call x1, Pallas kernels, attend(): pl.pallas_call(functools.partial(attend_kernel, len(pieces)), grid_spec=p...  33.2 us
    pallas_call x1, Pallas kernels, middle_first(): pl.pallas_call(functools.partial(middle_first_kernel, wide, len(pieces)),...  28.6 us
    ppermute x16, waiting for transfers between devices, over_core(): return lax.ppermute(values, 'narrow', narrow_perm(False, True))  16.7 us
    pallas_call x11, Pallas kernels, held_call(): pl.pallas_call(kernel, in_specs=[pl.BlockSpec(memory_space=pltpu.SMEM)] +...  15.8 us
  transfers between devices with their start and end apart: 51, of which 22 were waited for; matrix products, arithmetic and copies ran while one was open for 3% of the time, Pallas kernels for 47%

profile of v1, /device:TPU:0, one launch (start us, length us, event | category | flops | bytes accessed | tf_op | source)
XLA Modules:
  0.0 358.0 jit_solution(15540199928553324898)
XLA Ops:
  1.3 3.8 %pick.1 = (bf16[2,48,768]{2,1,0:T(8,128)(2,1)}, bf16[1,48,768]{2,1,0:T(8,128)(2,1)}, bf16[528,256]{1,0:T(8,128)(2,1)}, bf16[768,256]{1,0:T(8,128)(2,1)}) custom-call(s32[4]{0:T(128)} %pad_add_fusion.place, f32[3,96,768]{2,1,0:T(8,128)} %inward.1, f32[96,768]{1,0:T(8,128)} %out.1, f32[96,3072]{1,0:T(8,128)} %up.1, f32[384,768]{1,0:T(8,128)} %down.1), custom_call_target="tpu_custom_call" | custom-call | flops 1000000 | bytes 100000 | tf_op jit(solution)/shard_map/pick/pallas_call | solution.py:1015
  5.1 4.0 %collective-permute-start.4 = (bf16[1,48,768]{2,1,0:T(8,128)(2,1)}, bf16[1,48,768]{2,1,0:T(8,128)(2,1)S(1)}, u32[]{:S(2)}, u32[]{:S(2)}) collective-permute-start(bf16[1,48,768]{2,1,0:T(8,128)(2,1)} %get-tuple-element.178), channel_id=1, source_target_pairs={{0,16},{4,20},{8,24},{12,28},{16,0},{20,4},{24,8},{28,12},{1,17},{... | collective-permute-start | bytes 221192 | tf_op jit(solution)/shard_map/ppermute | solution.py:968
  16.2 3.1 multiply_sine_fusion
  21.1 5.1 %collective-permute-done.1 = bf16[2,48,768]{2,1,0:T(8,128)(2,1)S(1)} collective-permute-done((bf16[2,48,768]{2,1,0:T(8,128)(2,1)}, bf16[2,48,768]{2,1,0:T(8,128)(2,1)S(1)}, u32[]{:S(2)}, u32[]{:S(2)}) %collective-permute-start.1) | collective-permute-done | bytes 147488 | tf_op jit(solution)/shard_map/ppermute | solution.py:968
  31.5 3.2 collective-permute-start.9
  35.3 6.4 %collective-permute-done.8 = bf16[528,256]{1,0:T(8,128)(2,1)S(1)} collective-permute-done((bf16[528,256]{1,0:T(8,128)(2,1)S(1)}, bf16[528,256]{1,0:T(8,128)(2,1)S(1)}, u32[]{:S(2)}, u32[]{:S(2)}) %collective-permute-start.8) | collective-permute-done | bytes 270368 | tf_op jit(solution)/shard_map/ppermute | solution.py:968
  41.6 10.4 %collective-permute-done.9 = bf16[528,256]{1,0:T(8,128)(2,1)S(1)} collective-permute-done((bf16[528,256]{1,0:T(8,128)(2,1)S(1)}, bf16[528,256]{1,0:T(8,128)(2,1)S(1)}, u32[]{:S(2)}, u32[]{:S(2)}) %collective-permute-start.9) | collective-permute-done | bytes 270368 | tf_op jit(solution)/shard_map/ppermute | solution.py:968
  57.5 6.3 %collective-permute-start.17 = (bf16[768,256]{1,0:T(8,128)(2,1)}, bf16[768,256]{1,0:T(8,128)(2,1)}, u32[]{:S(2)}, u32[]{:S(2)}) collective-permute-start(bf16[768,256]{1,0:T(8,128)(2,1)} %get-tuple-element.203), channel_id=1, source_target_pairs={{0,8},{4,12},{8,16},{12,20},{16,24},{20,28},{24,0},{28,4},{1,9},{5... | collective-permute-start | bytes 1179656 | tf_op jit(solution)/shard_map/ppermute | solution.py:968
  67.6 33.2 %attend.1 = (bf16[1024,768]{1,0:T(8,128)(2,1)}, f32[3,1024,256]{2,1,0:T(8,128)}, bf16[768,1024]{1,0:T(8,128)(2,1)}, bf16[8,288,768]{2,1,0:T(8,128)(2,1)}, f32[3,...) custom-call(s32[1,24]{1,0:T(1,128)} %lengths.3, ...), custom_call_target="tpu_custom_call" | custom-call | flops 1000000 | bytes 100000 | tf_op jit(solution)/shard_map/attend/pallas_call | solution.py:317
  107.2 28.6 %middle_first.1 = (f32[1024,768]{1,0:T(8,128)}, bf16[1024,768]{1,0:T(8,128)(2,1)}, bf16[768,1024]{1,0:T(8,128)(2,1)}, bf16[768,1024]{1,0:T(8,128)(2,1)}, f32[102...) custom-call(s32[4]{0:T(128)} %pad_add_fusion.place, ...), custom_call_target="tpu_custom_call" | custom-call | flops 1000000 | bytes 100000 | tf_op jit(solution)/shard_map/middle_first/pallas_call | solution.py:793
  135.9 5.9 %collective-permute-done.21.refs_1_ = bf16[4,768,256]{2,1,0:T(8,128)(2,1)} collective-permute-done((bf16[4,768,256]{2,1,0:T(8,128)(2,1)S(1)}, bf16[4,768,256]{2,1,0:T(8,128)(2,1)}, u32[]{:S(2)}, u32[]{:S(2)}) %collective-permute-start.21) | collective-permute-done | bytes 1572896 | tf_op jit(solution)/shard_map/ppermute | solution.py:972
  143.4 3.1 collective-permute-done.23.refs_3_
  147.7 47.8 %middle_rest.1 = (f32[1024,768]{1,0:T(8,128)}, f32[1024,768]{1,0:T(8,128)}, f32[1024,768]{1,0:T(8,128)}, bf16[8,144,256]{2,1,0:T(8,128)(2,1)S(1)}, bf16[8,144,25...) custom-call(s32[4]{0:T(128)} %pad_add_fusion.place, ...), custom_call_target="tpu_custom_call" | custom-call | flops 1000000 | bytes 100000 | tf_op jit(solution)/shard_map/middle_rest/pallas_call | solution.py:832
  196.2 6.0 %collective-permute-done.26.refs_3_ = bf16[8,144,256]{2,1,0:T(8,128)(2,1)S(1)} collective-permute-done((bf16[8,144,256]{2,1,0:T(8,128)(2,1)S(1)}, bf16[8,144,256]{2,1,0:T(8,128)(2,1)S(1)}, u32[]{:S(2)}, u32[]{:S(2)}) %collective-permute-start.26) | collective-permute-done | bytes 589856 | tf_op jit(solution)/shard_map/ppermute | solution.py:984
  211.5 44.6 %attend_back.1 = (bf16[3,8,144,256]{3,2,1,0:T(8,128)(2,1)S(1)}, bf16[3,8,144,256]{3,2,1,0:T(8,128)(2,1)S(1)}, f32[3,1,768]{2,1,0:T(1,128)S(1)}, f32[1024,768]{1,0:T(8,128)}) custom-call(s32[1,24]{1,0:T(1,128)S(1)} %copy-done.12, s32[4]{0:T(128)S(1)} %copy-done.7, f32[1024,768]{1,0:T(8,128)} %get-tuple-element.240.dmixed_ref, ...), custom_call_target="tpu_custom_call" | custom-call | flops 1000000 | bytes 100000 | tf_op jit(solution)/shard_map/attend_back/pallas_call | solution.py:504
  261.0 3.1 collective-permute-start.32
  272.2 6.4 %input_side.1 = (f32[1024,768]{1,0:T(8,128)}, f32[16,768]{1,0:T(8,128)}) custom-call(bf16[1024,768]{1,0:T(8,128)(2,1)} %x_ref.1, f32[1024,768]{1,0:T(8,128)} %get-tuple-element.268.dx1_ref, f32[1024,768]{1,0:T(8,128)} %get-tuple-element.269.da1_ref, f32[13,768]{1,0:T(8,128)} %vectors.1, f32[8,768]{1,0:T(8,128)} %get-tuple-element.270.middle_ref, ...), custom_call_target="tpu_custom_call" | custom-call | flops 1000000 | bytes 100000 | tf_op jit(solution)/shard_map/input_side/pallas_call | solution.py:904
  278.6 5.5 %collective-permute-done.32.got = bf16[8,432,128]{2,1,0:T(8,128)(2,1)S(1)} collective-permute-done((bf16[8,432,128]{2,1,0:T(8,128)(2,1)S(1)}, bf16[8,432,128]{2,1,0:T(8,128)(2,1)S(1)}, u32[]{:S(2)}, u32[]{:S(2)}) %collective-permute-start.32) | collective-permute-done | bytes 884768 | tf_op jit(solution)/shard_map/ppermute | solution.py:980
  284.8 3.9 %collective-permute-start.37 = (bf16[4,432,128]{2,1,0:T(8,128)(2,1)S(1)}, bf16[4,432,128]{2,1,0:T(8,128)(2,1)S(1)}, u32[]{:S(2)}, u32[]{:S(2)}) collective-permute-start(bf16[4,432,128]{2,1,0:T(8,128)(2,1)S(1)} %get-tuple-element.291), channel_id=1, source_target_pairs={{0,4},{4,0},{8,12},{12,8},{16,20},{20,16},{24,28},{28,24},{1,5},{5... | collective-permute-start | bytes 1327112 | tf_op jit(solution)/shard_map/ppermute | solution.py:972
  288.8 6.0 %collective-permute-done.33.refs_1_ = bf16[768,256]{1,0:T(8,128)(2,1)} collective-permute-done((bf16[768,256]{1,0:T(8,128)(2,1)S(1)}, bf16[768,256]{1,0:T(8,128)(2,1)}, u32[]{:S(2)}, u32[]{:S(2)}) %collective-permute-start.33) | collective-permute-done | bytes 393248 | tf_op jit(solution)/shard_map/ppermute | solution.py:968
  296.3 2.5 collective-permute-done.37.got_ref
  301.0 3.8 %collective-permute-start.39 = (bf16[432,128]{1,0:T(8,128)(2,1)S(1)}, bf16[432,128]{1,0:T(8,128)(2,1)S(1)}, u32[]{:S(2)}, u32[]{:S(2)}) collective-permute-start(bf16[432,128]{1,0:T(8,128)(2,1)S(1)} %get-tuple-element.301), channel_id=1, source_target_pairs={{0,8},{4,12},{8,16},{12,20},{16,24},{20,28},{24,0},{28,4},{1,9},{5... | collective-permute-start | bytes 331784 | tf_op jit(solution)/shard_map/ppermute | solution.py:968
  306.3 3.1 collective-permute-start.41
  309.4 4.1 %collective-permute-done.40.refs_2_ = bf16[432,128]{1,0:T(8,128)(2,1)S(1)} collective-permute-done((bf16[432,128]{1,0:T(8,128)(2,1)S(1)}, bf16[432,128]{1,0:T(8,128)(2,1)S(1)}, u32[]{:S(2)}, u32[]{:S(2)}) %collective-permute-start.40) | collective-permute-done | bytes 110624 | tf_op jit(solution)/shard_map/ppermute | solution.py:968
  318.9 3.0 ffn_moments.1
  321.9 2.8 collective-permute-done.43
  329.2 4.0 %collective-permute-done.48 = f32[40,768]{1,0:T(8,128)S(1)} collective-permute-done((f32[40,768]{1,0:T(8,128)S(1)}, f32[40,768]{1,0:T(8,128)S(1)}, u32[]{:S(2)}, u32[]{:S(2)}) %collective-permute-start.48) | collective-permute-done | bytes 122912 | tf_op jit(solution)/shard_map/ppermute | solution.py:999
  333.3 6.4 %collective-permute-start.49 = (f32[40,768]{1,0:T(8,128)S(1)}, f32[40,768]{1,0:T(8,128)S(1)}, u32[]{:S(2)}, u32[]{:S(2)}) collective-permute-start(f32[40,768]{1,0:T(8,128)S(1)} %add.28), channel_id=1, source_target_pairs={{0,8},{4,12},{8,0},{12,4},{16,24},{20,28},{24,16},{28,20},{1,9},{5... | collective-permute-start | bytes 368648 | tf_op jit(solution)/shard_map/ppermute | solution.py:999
  339.7 3.2 collective-permute-done.49
  342.9 2.6 collective-permute-start.50
  347.3 3.6 collective-permute-done.50
  351.5 6.2 %finish.1 = (f32[3,768]{1,0:T(4,128)}, f32[3072]{0:T(1024)}, f32[768]{0:T(1024)}, f32[768]{0:T(1024)}, f32[3,96,768]{2,1,0:T(8,128)}, /*index=5*/f32[96,3072]{1,...) custom-call(s32[4]{0:T(128)} %pad_add_fusion.place, ...), custom_call_target="tpu_custom_call" | custom-call | flops 1000000 | bytes 100000 | tf_op jit(solution)/shard_map/finish/pallas_call | solution.py:1015
  (213 shorter events, 74.6 us)
Async XLA Ops:
  5.1 14.9 %collective-permute-start.4 = (bf16[1,48,768]{2,1,0:T(8,128)(2,1)}, bf16[1,48,768]{2,1,0:T(8,128)(2,1)S(1)}, u32[]{:S(2)}, u32[]{:S(2)}) collective-permute-start(bf16[1,48,768]{2,1,0:T(8,128)(2,1)} %get-tuple-element.178), channel_id=1, source_target_pairs={{0,16},{4,20},{8,24},{12,28},{16,0},{20,4},{24,8},{28,12},{1,17},{... | collective-permute-start | bytes 221192 | tf_op jit(solution)/shard_map/ppermute | solution.py:968
  9.1 11.9 %collective-permute-start.5 = (bf16[1,48,768]{2,1,0:T(8,128)(2,1)}, bf16[1,48,768]{2,1,0:T(8,128)(2,1)S(1)}, u32[]{:S(2)}, u32[]{:S(2)}) collective-permute-start(bf16[1,48,768]{2,1,0:T(8,128)(2,1)} %get-tuple-element.178), channel_id=1, source_target_pairs={{0,24},{4,28},{8,0},{12,4},{16,8},{20,12},{24,16},{28,20},{1,25},{... | collective-permute-start | bytes 221192 | tf_op jit(solution)/shard_map/ppermute | solution.py:968
  10.5 10.6 %collective-permute-start.3 = (bf16[1,48,768]{2,1,0:T(8,128)(2,1)}, bf16[1,48,768]{2,1,0:T(8,128)(2,1)S(1)}, u32[]{:S(2)}, u32[]{:S(2)}) collective-permute-start(bf16[1,48,768]{2,1,0:T(8,128)(2,1)} %get-tuple-element.178), channel_id=1, source_target_pairs={{0,8},{4,12},{8,16},{12,20},{16,24},{20,28},{24,0},{28,4},{1,9},{5... | collective-permute-start | bytes 221192 | tf_op jit(solution)/shard_map/ppermute | solution.py:968
  11.1 10.0 %collective-permute-start = (bf16[2,48,768]{2,1,0:T(8,128)(2,1)}, bf16[2,48,768]{2,1,0:T(8,128)(2,1)S(1)}, u32[]{:S(2)}, u32[]{:S(2)}) collective-permute-start(bf16[2,48,768]{2,1,0:T(8,128)(2,1)} %get-tuple-element.177), channel_id=1, source_target_pairs={{0,8},{4,12},{8,16},{12,20},{16,24},{20,28},{24,0},{28,4},{1,9},{5... | collective-permute-start | bytes 442376 | tf_op jit(solution)/shard_map/ppermute | solution.py:968
  12.7 13.6 %collective-permute-start.1 = (bf16[2,48,768]{2,1,0:T(8,128)(2,1)}, bf16[2,48,768]{2,1,0:T(8,128)(2,1)S(1)}, u32[]{:S(2)}, u32[]{:S(2)}) collective-permute-start(bf16[2,48,768]{2,1,0:T(8,128)(2,1)} %get-tuple-element.177), channel_id=1, source_target_pairs={{0,16},{4,20},{8,24},{12,28},{16,0},{20,4},{24,8},{28,12},{1,17},{... | collective-permute-start | bytes 442376 | tf_op jit(solution)/shard_map/ppermute | solution.py:968
  27.5 24.7 %collective-permute-start.6 = (bf16[4,2,48,768]{3,2,1,0:T(8,128)(2,1)S(1)}, bf16[4,2,48,768]{3,2,1,0:T(8,128)(2,1)S(1)}, u32[]{:S(2)}, u32[]{:S(2)}) collective-permute-start(bf16[4,2,48,768]{3,2,1,0:T(8,128)(2,1)S(1)} %pad_maximum_fusion.2.refs_0_), channel_id=1, source_target_pairs={{0,4},{4,0},{8,12},{12,8},{16,20},{20,16},{24,28},{28,24},{1,5},{5... | collective-permute-start | bytes 1769480 | tf_op jit(solution)/shard_map/ppermute | solution.py:972
  29.3 12.3 %collective-permute-start.8 = (bf16[528,256]{1,0:T(8,128)(2,1)S(1)}, bf16[528,256]{1,0:T(8,128)(2,1)S(1)}, u32[]{:S(2)}, u32[]{:S(2)}) collective-permute-start(bf16[528,256]{1,0:T(8,128)(2,1)S(1)} %copy-done.32), channel_id=1, source_target_pairs={{0,8},{4,12},{8,16},{12,20},{16,24},{20,28},{24,0},{28,4},{1,9},{5... | collective-permute-start | bytes 811016 | tf_op jit(solution)/shard_map/ppermute | solution.py:968
  31.5 20.6 %collective-permute-start.9 = (bf16[528,256]{1,0:T(8,128)(2,1)S(1)}, bf16[528,256]{1,0:T(8,128)(2,1)S(1)}, u32[]{:S(2)}, u32[]{:S(2)}) collective-permute-start(bf16[528,256]{1,0:T(8,128)(2,1)S(1)} %copy-done.32), channel_id=1, source_target_pairs={{0,16},{4,20},{8,24},{12,28},{16,0},{20,4},{24,8},{28,12},{1,17},{... | collective-permute-start | bytes 811016 | tf_op jit(solution)/shard_map/ppermute | solution.py:968
  34.7 17.4 %collective-permute-start.10 = (bf16[528,256]{1,0:T(8,128)(2,1)S(1)}, bf16[528,256]{1,0:T(8,128)(2,1)S(1)}, u32[]{:S(2)}, u32[]{:S(2)}) collective-permute-start(bf16[528,256]{1,0:T(8,128)(2,1)S(1)} %copy-done.32), channel_id=1, source_target_pairs={{0,24},{4,28},{8,0},{12,4},{16,8},{20,12},{24,16},{28,20},{1,25},{... | collective-permute-start | bytes 811016 | tf_op jit(solution)/shard_map/ppermute | solution.py:968
  34.7 17.5 %collective-permute-start.7 = (bf16[4,1,48,768]{3,2,1,0:T(8,128)(2,1)S(1)}, bf16[4,1,48,768]{3,2,1,0:T(8,128)(2,1)S(1)}, u32[]{:S(2)}, u32[]{:S(2)}) collective-permute-start(bf16[4,1,48,768]{3,2,1,0:T(8,128)(2,1)S(1)} %pad_maximum_fusion.4.refs_4_), channel_id=1, source_target_pairs={{0,4},{4,0},{8,12},{12,8},{16,20},{20,16},{24,28},{28,24},{1,5},{5... | collective-permute-start | bytes 884744 | tf_op jit(solution)/shard_map/ppermute | solution.py:972
  57.0 43.9 %collective-permute-start.16 = (bf16[4,528,256]{2,1,0:T(8,128)(2,1)S(1)}, bf16[4,528,256]{2,1,0:T(8,128)(2,1)}, u32[]{:S(2)}, u32[]{:S(2)}) collective-permute-start(bf16[4,528,256]{2,1,0:T(8,128)(2,1)S(1)} %pad_maximum_fusion.1.refs_0_), channel_id=1, source_target_pairs={{0,4},{4,0},{8,12},{12,8},{16,20},{20,16},{24,28},{28,24},{1,5},{5... | collective-permute-start | bytes 3244040 | tf_op jit(solution)/shard_map/ppermute | solution.py:972
  57.5 43.4 %collective-permute-start.17 = (bf16[768,256]{1,0:T(8,128)(2,1)}, bf16[768,256]{1,0:T(8,128)(2,1)}, u32[]{:S(2)}, u32[]{:S(2)}) collective-permute-start(bf16[768,256]{1,0:T(8,128)(2,1)} %get-tuple-element.203), channel_id=1, source_target_pairs={{0,8},{4,12},{8,16},{12,20},{16,24},{20,28},{24,0},{28,4},{1,9},{5... | collective-permute-start | bytes 1179656 | tf_op jit(solution)/shard_map/ppermute | solution.py:968
  63.8 37.1 %collective-permute-start.18 = (bf16[768,256]{1,0:T(8,128)(2,1)}, bf16[768,256]{1,0:T(8,128)(2,1)}, u32[]{:S(2)}, u32[]{:S(2)}) collective-permute-start(bf16[768,256]{1,0:T(8,128)(2,1)} %get-tuple-element.203), channel_id=1, source_target_pairs={{0,16},{4,20},{8,24},{12,28},{16,0},{20,4},{24,8},{28,12},{1,17},{... | collective-permute-start | bytes 1179656 | tf_op jit(solution)/shard_map/ppermute | solution.py:968
  63.8 37.1 %collective-permute-start.19 = (bf16[768,256]{1,0:T(8,128)(2,1)}, bf16[768,256]{1,0:T(8,128)(2,1)}, u32[]{:S(2)}, u32[]{:S(2)}) collective-permute-start(bf16[768,256]{1,0:T(8,128)(2,1)} %get-tuple-element.203), channel_id=1, source_target_pairs={{0,24},{4,28},{8,0},{12,4},{16,8},{20,12},{24,16},{28,20},{1,25},{... | collective-permute-start | bytes 1179656 | tf_op jit(solution)/shard_map/ppermute | solution.py:968
  67.6 35.4 %collective-permute-start.15 = (bf16[4,528,256]{2,1,0:T(8,128)(2,1)S(1)}, bf16[4,528,256]{2,1,0:T(8,128)(2,1)}, u32[]{:S(2)}, u32[]{:S(2)}) collective-permute-start(bf16[4,528,256]{2,1,0:T(8,128)(2,1)S(1)} %pad_maximum_fusion.1.refs_0_), channel_id=1, source_target_pairs={{0,1},{1,0},{2,3},{3,2},{4,5},{5,4},{6,7},{7,6},{8,9},{9,8},{10,11... | collective-permute-start | bytes 3244040 | tf_op jit(solution)/shard_map/ppermute | solution.py:984
  105.0 36.8 %collective-permute-start.21 = (bf16[4,768,256]{2,1,0:T(8,128)(2,1)S(1)}, bf16[4,768,256]{2,1,0:T(8,128)(2,1)}, u32[]{:S(2)}, u32[]{:S(2)}) collective-permute-start(bf16[4,768,256]{2,1,0:T(8,128)(2,1)S(1)} %pad_maximum_fusion.refs_0_), channel_id=1, source_target_pairs={{0,4},{4,0},{8,12},{12,8},{16,20},{20,16},{24,28},{28,24},{1,5},{5... | collective-permute-start | bytes 4718600 | tf_op jit(solution)/shard_map/ppermute | solution.py:972
  106.5 35.3 %collective-permute-start.22 = (bf16[4,768,256]{2,1,0:T(8,128)(2,1)S(1)}, bf16[4,768,256]{2,1,0:T(8,128)(2,1)S(1)}, u32[]{:S(2)}, u32[]{:S(2)}) collective-permute-start(bf16[4,768,256]{2,1,0:T(8,128)(2,1)S(1)} %pad_maximum_fusion.refs_0_), channel_id=1, source_target_pairs={{0,1},{1,0},{2,3},{3,2},{4,5},{5,4},{6,7},{7,6},{8,9},{9,8},{10,11... | collective-permute-start | bytes 4718600 | tf_op jit(solution)/shard_map/ppermute | solution.py:984
  142.9 52.6 %collective-permute-start.24 = (bf16[8,384,256]{2,1,0:T(8,128)(2,1)}, bf16[8,384,256]{2,1,0:T(8,128)(2,1)S(1)}, u32[]{:S(2)}, u32[]{:S(2)}) collective-permute-start(bf16[8,384,256]{2,1,0:T(8,128)(2,1)} %get-tuple-element.226), channel_id=1, source_target_pairs={{0,1},{1,0},{2,3},{3,2},{4,5},{5,4},{6,7},{7,6},{8,9},{9,8},{10,11... | collective-permute-start | bytes 4718600 | tf_op jit(solution)/shard_map/ppermute | solution.py:984
  206.0 50.1 %collective-permute-start.27 = (bf16[4,768,256]{2,1,0:T(8,128)(2,1)}, bf16[4,768,256]{2,1,0:T(8,128)(2,1)S(1)}, u32[]{:S(2)}, u32[]{:S(2)}) collective-permute-start(bf16[4,768,256]{2,1,0:T(8,128)(2,1)} %get-tuple-element.252), channel_id=1, source_target_pairs={{0,4},{4,0},{8,12},{12,8},{16,20},{20,16},{24,28},{28,24},{1,5},{5... | collective-permute-start | bytes 4718600 | tf_op jit(solution)/shard_map/ppermute | solution.py:972
  207.5 48.6 %collective-permute-start.28 = (bf16[2,528,256]{2,1,0:T(8,128)(2,1)S(1)}, bf16[2,528,256]{2,1,0:T(8,128)(2,1)S(1)}, u32[]{:S(2)}, u32[]{:S(2)}) collective-permute-start(bf16[2,528,256]{2,1,0:T(8,128)(2,1)S(1)} %get-tuple-element.253), channel_id=1, source_target_pairs={{0,8},{4,12},{8,16},{12,20},{16,24},{20,28},{24,0},{28,4},{1,9},{5... | collective-permute-start | bytes 1622024 | tf_op jit(solution)/shard_map/ppermute | solution.py:968
  209.1 47.0 %collective-permute-start.29 = (bf16[2,528,256]{2,1,0:T(8,128)(2,1)S(1)}, bf16[2,528,256]{2,1,0:T(8,128)(2,1)S(1)}, u32[]{:S(2)}, u32[]{:S(2)}) collective-permute-start(bf16[2,528,256]{2,1,0:T(8,128)(2,1)S(1)} %get-tuple-element.254), channel_id=1, source_target_pairs={{0,16},{4,20},{8,24},{12,28},{16,0},{20,4},{24,8},{28,12},{1,17},{... | collective-permute-start | bytes 1622024 | tf_op jit(solution)/shard_map/ppermute | solution.py:968
  210.8 45.3 %collective-permute-start.30 = (bf16[2,528,256]{2,1,0:T(8,128)(2,1)S(1)}, bf16[2,528,256]{2,1,0:T(8,128)(2,1)S(1)}, u32[]{:S(2)}, u32[]{:S(2)}) collective-permute-start(bf16[2,528,256]{2,1,0:T(8,128)(2,1)S(1)} %get-tuple-element.255), channel_id=1, source_target_pairs={{0,24},{4,28},{8,0},{12,4},{16,8},{20,12},{24,16},{28,20},{1,25},{... | collective-permute-start | bytes 1622024 | tf_op jit(solution)/shard_map/ppermute | solution.py:968
  261.0 23.1 %collective-permute-start.32 = (bf16[8,432,128]{2,1,0:T(8,128)(2,1)S(1)}, bf16[8,432,128]{2,1,0:T(8,128)(2,1)S(1)}, u32[]{:S(2)}, u32[]{:S(2)}) collective-permute-start(bf16[8,432,128]{2,1,0:T(8,128)(2,1)S(1)} %get-tuple-element.267), channel_id=1, source_target_pairs={{0,2},{1,3},{2,0},{3,1},{4,6},{5,7},{6,4},{7,5},{8,10},{9,11},{10,... | collective-permute-start | bytes 2654216 | tf_op jit(solution)/shard_map/ppermute | solution.py:980
  264.1 24.6 %collective-permute-start.34 = (bf16[768,256]{1,0:T(8,128)(2,1)}, bf16[768,256]{1,0:T(8,128)(2,1)}, u32[]{:S(2)}, u32[]{:S(2)}) collective-permute-start(bf16[768,256]{1,0:T(8,128)(2,1)} %get-tuple-element.283), channel_id=1, source_target_pairs={{0,16},{4,20},{8,24},{12,28},{16,0},{20,4},{24,8},{28,12},{1,17},{... | collective-permute-start | bytes 1179656 | tf_op jit(solution)/shard_map/ppermute | solution.py:968
  266.1 22.7 %collective-permute-start.35 = (bf16[768,256]{1,0:T(8,128)(2,1)}, bf16[768,256]{1,0:T(8,128)(2,1)}, u32[]{:S(2)}, u32[]{:S(2)}) collective-permute-start(bf16[768,256]{1,0:T(8,128)(2,1)} %get-tuple-element.284), channel_id=1, source_target_pairs={{0,24},{4,28},{8,0},{12,4},{16,8},{20,12},{24,16},{28,20},{1,25},{... | collective-permute-start | bytes 1179656 | tf_op jit(solution)/shard_map/ppermute | solution.py:968
  268.3 26.4 %collective-permute-start.33 = (bf16[768,256]{1,0:T(8,128)(2,1)S(1)}, bf16[768,256]{1,0:T(8,128)(2,1)}, u32[]{:S(2)}, u32[]{:S(2)}) collective-permute-start(bf16[768,256]{1,0:T(8,128)(2,1)S(1)} %get-tuple-element.282), channel_id=1, source_target_pairs={{0,8},{4,12},{8,16},{12,20},{16,24},{20,28},{24,0},{28,4},{1,9},{5... | collective-permute-start | bytes 1179656 | tf_op jit(solution)/shard_map/ppermute | solution.py:968
  271.0 17.8 %collective-permute-start.36 = (bf16[528,256]{1,0:T(8,128)(2,1)}, bf16[528,256]{1,0:T(8,128)(2,1)}, u32[]{:S(2)}, u32[]{:S(2)}) collective-permute-start(bf16[528,256]{1,0:T(8,128)(2,1)} %get-tuple-element.290), channel_id=1, source_target_pairs={{0,4},{4,0},{8,12},{12,8},{16,20},{20,16},{24,28},{28,24},{1,5},{5... | collective-permute-start | bytes 811016 | tf_op jit(solution)/shard_map/ppermute | solution.py:972
  284.8 14.0 %collective-permute-start.37 = (bf16[4,432,128]{2,1,0:T(8,128)(2,1)S(1)}, bf16[4,432,128]{2,1,0:T(8,128)(2,1)S(1)}, u32[]{:S(2)}, u32[]{:S(2)}) collective-permute-start(bf16[4,432,128]{2,1,0:T(8,128)(2,1)S(1)} %get-tuple-element.291), channel_id=1, source_target_pairs={{0,4},{4,0},{8,12},{12,8},{16,20},{20,16},{24,28},{28,24},{1,5},{5... | collective-permute-start | bytes 1327112 | tf_op jit(solution)/shard_map/ppermute | solution.py:972
  299.5 16.0 %collective-permute-start.38 = (bf16[1296,256]{1,0:T(8,128)(2,1)S(1)}, bf16[1296,256]{1,0:T(8,128)(2,1)S(1)}, u32[]{:S(2)}, u32[]{:S(2)}) collective-permute-start(bf16[1296,256]{1,0:T(8,128)(2,1)S(1)} %z_sum.2), channel_id=1, source_target_pairs={{0,2},{1,3},{2,0},{3,1},{4,6},{5,7},{6,4},{7,5},{8,10},{9,11},{10,... | collective-permute-start | bytes 1990664 | tf_op jit(solution)/shard_map/ppermute | solution.py:980
  304.8 8.7 %collective-permute-start.40 = (bf16[432,128]{1,0:T(8,128)(2,1)S(1)}, bf16[432,128]{1,0:T(8,128)(2,1)S(1)}, u32[]{:S(2)}, u32[]{:S(2)}) collective-permute-start(bf16[432,128]{1,0:T(8,128)(2,1)S(1)} %get-tuple-element.302), channel_id=1, source_target_pairs={{0,16},{4,20},{8,24},{12,28},{16,0},{20,4},{24,8},{28,12},{1,17},{... | collective-permute-start | bytes 331784 | tf_op jit(solution)/shard_map/ppermute | solution.py:968
  315.8 8.9 %collective-permute-start.42 = (f32[432,128]{1,0:T(8,128)S(1)}, f32[432,128]{1,0:T(8,128)S(1)}, u32[]{:S(2)}, u32[]{:S(2)}) collective-permute-start(f32[432,128]{1,0:T(8,128)S(1)} %z_sum.3.own), channel_id=1, source_target_pairs={{0,2},{1,3},{2,0},{3,1},{4,6},{5,7},{6,4},{7,5},{8,10},{9,11},{10,... | collective-permute-start | bytes 663560 | tf_op jit(solution)/shard_map/ppermute | solution.py:980
  333.3 9.6 %collective-permute-start.49 = (f32[40,768]{1,0:T(8,128)S(1)}, f32[40,768]{1,0:T(8,128)S(1)}, u32[]{:S(2)}, u32[]{:S(2)}) collective-permute-start(f32[40,768]{1,0:T(8,128)S(1)} %add.28), channel_id=1, source_target_pairs={{0,8},{4,12},{8,0},{12,4},{16,24},{20,28},{24,16},{28,20},{1,9},{5... | collective-permute-start | bytes 368648 | tf_op jit(solution)/shard_map/ppermute | solution.py:999
  (61 other events, 698.1 us)

commit v2 on v1

--- a/solution.py
+++ b/solution.py
@@ -761,7 +761,7 @@
             vec_ref[3:4, :] += jnp.sum(dy, axis=0, keepdims=True)
             dmixed_ref[here, :] = mm_nt(low, out_ref[...])
 
-        row_blocks(last_rows, True)
+        row_blocks(last_rows)
         for cols in range(0, D, 256):
             up[cols : cols + 256, :] = transposed(attn_ref[:, cols : cols + 256])
         store_halves(mm(up[...], dbranch[...]).astype(BF16), place[3], okeep_ref, osend_ref)

time: 363 us -> 361 us (level)
    ppermute x7, starting transfers between devices: 10.9 us -> 3.59 us  [over_x(): return lax.ppermute(values, 'wide', wide_perm(0, True))]
    ppermute x16, starting transfers between devices: 3.46 us -> 8.6 us  [over_core(): return lax.ppermute(values, 'narrow', narrow_perm(False, True))]
    ppermute x21, waiting for transfers between devices: 33.2 us -> 37.5 us  [over_z(): return lax.ppermute(values, 'wide', wide_perm(shift, False))]
  transfers between devices with their start and end apart: 51 -> 51, of which waited for: 22 -> 21; matrix products, arithmetic and copies ran while one was open for 3% -> 3% of each run, Pallas kernels for 47% -> 47%
where the time goes in v2:
time: 361 us; the launch traced here: 357 us
  Pallas kernels  186 us (52%)
  waiting for transfers between devices  80.3 us (22%)
  starting transfers between devices  71.2 us (20%)
  other arithmetic  9.8 us (3%)
  local copies, waits for them, and re-layouts  8.54 us (2%)
    pallas_call x1, Pallas kernels, middle_rest(): pl.pallas_call(functools.partial(middle_rest_kernel, wide, len(pieces)),...  47 us
    pallas_call x1, Pallas kernels, attend_back(): pl.pallas_call(attend_back_kernel, grid_spec=pltpu.PrefetchScalarGridSpec...  44.4 us
    ppermute x21, starting transfers between devices, over_z(): return lax.ppermute(values, 'wide', wide_perm(shift, False))  43.1 us
    ppermute x21, waiting for transfers between devices, over_z(): return lax.ppermute(values, 'wide', wide_perm(shift, False))  37.5 us
    pallas_call x1, Pallas kernels, attend(): pl.pallas_call(functools.partial(attend_kernel, len(pieces)), grid_spec=p...  33.3 us
    pallas_call x1, Pallas kernels, middle_first(): pl.pallas_call(functools.partial(middle_first_kernel, wide, len(pieces)),...  28.7 us
    ppermute x16, waiting for transfers between devices, over_core(): return lax.ppermute(values, 'narrow', narrow_perm(False, True))  16.3 us
    pallas_call x11, Pallas kernels, held_call(): pl.pallas_call(kernel, in_specs=[pl.BlockSpec(memory_space=pltpu.SMEM)] +...  15.8 us
  transfers between devices with their start and end apart: 51, of which 21 were waited for; matrix products, arithmetic and copies ran while one was open for 3% of the time, Pallas kernels for 47%

profile of v2, /device:TPU:0, one launch (start us, length us, event | category | flops | bytes accessed | tf_op | source)
XLA Modules:
  0.0 357.2 jit_solution(11899981273886186018)
XLA Ops:
  1.3 3.8 %pick.1 = (bf16[2,48,768]{2,1,0:T(8,128)(2,1)}, bf16[1,48,768]{2,1,0:T(8,128)(2,1)}, bf16[528,256]{1,0:T(8,128)(2,1)}, bf16[768,256]{1,0:T(8,128)(2,1)}) custom-call(s32[4]{0:T(128)} %pad_add_fusion.place, f32[3,96,768]{2,1,0:T(8,128)} %inward.1, f32[96,768]{1,0:T(8,128)} %out.1, f32[96,3072]{1,0:T(8,128)} %up.1, f32[384,768]{1,0:T(8,128)} %down.1), custom_call_target="tpu_custom_call" | custom-call | flops 1000000 | bytes 100000 | tf_op jit(solution)/shard_map/pick/pallas_call | solution.py:1015
  5.1 4.0 %collective-permute-start.4 = (bf16[1,48,768]{2,1,0:T(8,128)(2,1)}, bf16[1,48,768]{2,1,0:T(8,128)(2,1)S(1)}, u32[]{:S(2)}, u32[]{:S(2)}) collective-permute-start(bf16[1,48,768]{2,1,0:T(8,128)(2,1)} %get-tuple-element.178), channel_id=1, source_target_pairs={{0,16},{4,20},{8,24},{12,28},{16,0},{20,4},{24,8},{28,12},{1,17},{... | collective-permute-start | bytes 221192 | tf_op jit(solution)/shard_map/ppermute | solution.py:968
  16.2 3.1 multiply_sine_fusion
  21.1 5.1 %collective-permute-done.1 = bf16[2,48,768]{2,1,0:T(8,128)(2,1)S(1)} collective-permute-done((bf16[2,48,768]{2,1,0:T(8,128)(2,1)}, bf16[2,48,768]{2,1,0:T(8,128)(2,1)S(1)}, u32[]{:S(2)}, u32[]{:S(2)}) %collective-permute-start.1) | collective-permute-done | bytes 147488 | tf_op jit(solution)/shard_map/ppermute | solution.py:968
  31.5 3.2 collective-permute-start.9
  35.3 6.4 %collective-permute-done.8 = bf16[528,256]{1,0:T(8,128)(2,1)S(1)} collective-permute-done((bf16[528,256]{1,0:T(8,128)(2,1)S(1)}, bf16[528,256]{1,0:T(8,128)(2,1)S(1)}, u32[]{:S(2)}, u32[]{:S(2)}) %collective-permute-start.8) | collective-permute-done | bytes 270368 | tf_op jit(solution)/shard_map/ppermute | solution.py:968
  41.6 10.4 %collective-permute-done.9 = bf16[528,256]{1,0:T(8,128)(2,1)S(1)} collective-permute-done((bf16[528,256]{1,0:T(8,128)(2,1)S(1)}, bf16[528,256]{1,0:T(8,128)(2,1)S(1)}, u32[]{:S(2)}, u32[]{:S(2)}) %collective-permute-start.9) | collective-permute-done | bytes 270368 | tf_op jit(solution)/shard_map/ppermute | solution.py:968
  57.5 6.3 %collective-permute-start.17 = (bf16[768,256]{1,0:T(8,128)(2,1)}, bf16[768,256]{1,0:T(8,128)(2,1)}, u32[]{:S(2)}, u32[]{:S(2)}) collective-permute-start(bf16[768,256]{1,0:T(8,128)(2,1)} %get-tuple-element.203), channel_id=1, source_target_pairs={{0,8},{4,12},{8,16},{12,20},{16,24},{20,28},{24,0},{28,4},{1,9},{5... | collective-permute-start | bytes 1179656 | tf_op jit(solution)/shard_map/ppermute | solution.py:968
  67.6 33.3 %attend.1 = (bf16[1024,768]{1,0:T(8,128)(2,1)}, f32[3,1024,256]{2,1,0:T(8,128)}, bf16[768,1024]{1,0:T(8,128)(2,1)}, bf16[8,288,768]{2,1,0:T(8,128)(2,1)}, f32[3,...) custom-call(s32[1,24]{1,0:T(1,128)} %lengths.3, ...), custom_call_target="tpu_custom_call" | custom-call | flops 1000000 | bytes 100000 | tf_op jit(solution)/shard_map/attend/pallas_call | solution.py:317
  108.0 28.7 %middle_first.1 = (f32[1024,768]{1,0:T(8,128)}, bf16[1024,768]{1,0:T(8,128)(2,1)}, bf16[768,1024]{1,0:T(8,128)(2,1)}, bf16[768,1024]{1,0:T(8,128)(2,1)}, f32[102...) custom-call(s32[4]{0:T(128)} %pad_add_fusion.place, ...), custom_call_target="tpu_custom_call" | custom-call | flops 1000000 | bytes 100000 | tf_op jit(solution)/shard_map/middle_first/pallas_call | solution.py:793
  136.7 7.1 %collective-permute-done.21.refs_1_ = bf16[4,768,256]{2,1,0:T(8,128)(2,1)} collective-permute-done((bf16[4,768,256]{2,1,0:T(8,128)(2,1)S(1)}, bf16[4,768,256]{2,1,0:T(8,128)(2,1)}, u32[]{:S(2)}, u32[]{:S(2)}) %collective-permute-start.21) | collective-permute-done | bytes 1572896 | tf_op jit(solution)/shard_map/ppermute | solution.py:972
  145.5 3.1 collective-permute-done.23.refs_3_
  149.7 47.0 %middle_rest.1 = (f32[1024,768]{1,0:T(8,128)}, f32[1024,768]{1,0:T(8,128)}, f32[1024,768]{1,0:T(8,128)}, bf16[8,144,256]{2,1,0:T(8,128)(2,1)S(1)}, bf16[8,144,25...) custom-call(s32[4]{0:T(128)} %pad_add_fusion.place, ...), custom_call_target="tpu_custom_call" | custom-call | flops 1000000 | bytes 100000 | tf_op jit(solution)/shard_map/middle_rest/pallas_call | solution.py:832
  197.3 6.0 %collective-permute-done.26.refs_3_ = bf16[8,144,256]{2,1,0:T(8,128)(2,1)S(1)} collective-permute-done((bf16[8,144,256]{2,1,0:T(8,128)(2,1)S(1)}, bf16[8,144,256]{2,1,0:T(8,128)(2,1)S(1)}, u32[]{:S(2)}, u32[]{:S(2)}) %collective-permute-start.26) | collective-permute-done | bytes 589856 | tf_op jit(solution)/shard_map/ppermute | solution.py:984
  207.4 3.7 %collective-permute-start.29 = (bf16[2,528,256]{2,1,0:T(8,128)(2,1)S(1)}, bf16[2,528,256]{2,1,0:T(8,128)(2,1)S(1)}, u32[]{:S(2)}, u32[]{:S(2)}) collective-permute-start(bf16[2,528,256]{2,1,0:T(8,128)(2,1)S(1)} %get-tuple-element.254), channel_id=1, source_target_pairs={{0,16},{4,20},{8,24},{12,28},{16,0},{20,4},{24,8},{28,12},{1,17},{... | collective-permute-start | bytes 1622024 | tf_op jit(solution)/shard_map/ppermute | solution.py:968
  211.3 44.4 %attend_back.1 = (bf16[3,8,144,256]{3,2,1,0:T(8,128)(2,1)S(1)}, bf16[3,8,144,256]{3,2,1,0:T(8,128)(2,1)S(1)}, f32[3,1,768]{2,1,0:T(1,128)S(1)}, f32[1024,768]{1,0:T(8,128)}) custom-call(s32[1,24]{1,0:T(1,128)S(1)} %copy-done.12, s32[4]{0:T(128)S(1)} %copy-done.7, f32[1024,768]{1,0:T(8,128)} %get-tuple-element.240.dmixed_ref, ...), custom_call_target="tpu_custom_call" | custom-call | flops 1000000 | bytes 100000 | tf_op jit(solution)/shard_map/attend_back/pallas_call | solution.py:504
  255.8 2.9 collective-permute-start.31
  266.5 3.6 collective-permute-start.35
  272.6 6.6 %input_side.1 = (f32[1024,768]{1,0:T(8,128)}, f32[16,768]{1,0:T(8,128)}) custom-call(bf16[1024,768]{1,0:T(8,128)(2,1)} %x_ref.1, f32[1024,768]{1,0:T(8,128)} %get-tuple-element.268.dx1_ref, f32[1024,768]{1,0:T(8,128)} %get-tuple-element.269.da1_ref, f32[13,768]{1,0:T(8,128)} %vectors.1, f32[8,768]{1,0:T(8,128)} %get-tuple-element.270.middle_ref, ...), custom_call_target="tpu_custom_call" | custom-call | flops 1000000 | bytes 100000 | tf_op jit(solution)/shard_map/input_side/pallas_call | solution.py:904
  279.2 5.9 %collective-permute-done.32.got = bf16[8,432,128]{2,1,0:T(8,128)(2,1)S(1)} collective-permute-done((bf16[8,432,128]{2,1,0:T(8,128)(2,1)S(1)}, bf16[8,432,128]{2,1,0:T(8,128)(2,1)S(1)}, u32[]{:S(2)}, u32[]{:S(2)}) %collective-permute-start.32) | collective-permute-done | bytes 884768 | tf_op jit(solution)/shard_map/ppermute | solution.py:980
  286.4 9.9 %collective-permute-done.33.refs_1_ = bf16[768,256]{1,0:T(8,128)(2,1)} collective-permute-done((bf16[768,256]{1,0:T(8,128)(2,1)S(1)}, bf16[768,256]{1,0:T(8,128)(2,1)}, u32[]{:S(2)}, u32[]{:S(2)}) %collective-permute-start.33) | collective-permute-done | bytes 393248 | tf_op jit(solution)/shard_map/ppermute | solution.py:968
  300.0 5.9 %collective-permute-start.39 = (bf16[432,128]{1,0:T(8,128)(2,1)S(1)}, bf16[432,128]{1,0:T(8,128)(2,1)S(1)}, u32[]{:S(2)}, u32[]{:S(2)}) collective-permute-start(bf16[432,128]{1,0:T(8,128)(2,1)S(1)} %get-tuple-element.301), channel_id=1, source_target_pairs={{0,8},{4,12},{8,16},{12,20},{16,24},{20,28},{24,0},{28,4},{1,9},{5... | collective-permute-start | bytes 331784 | tf_op jit(solution)/shard_map/ppermute | solution.py:968
  306.9 2.9 collective-permute-start.41
  309.8 4.1 %collective-permute-done.40.refs_2_ = bf16[432,128]{1,0:T(8,128)(2,1)S(1)} collective-permute-done((bf16[432,128]{1,0:T(8,128)(2,1)S(1)}, bf16[432,128]{1,0:T(8,128)(2,1)S(1)}, u32[]{:S(2)}, u32[]{:S(2)}) %collective-permute-start.40) | collective-permute-done | bytes 110624 | tf_op jit(solution)/shard_map/ppermute | solution.py:968
  317.9 3.0 ffn_moments.1
  320.9 2.8 collective-permute-done.43
  327.1 5.2 %collective-permute-done.48 = f32[40,768]{1,0:T(8,128)S(1)} collective-permute-done((f32[40,768]{1,0:T(8,128)S(1)}, f32[40,768]{1,0:T(8,128)S(1)}, u32[]{:S(2)}, u32[]{:S(2)}) %collective-permute-start.48) | collective-permute-done | bytes 122912 | tf_op jit(solution)/shard_map/ppermute | solution.py:999
  332.3 6.9 %collective-permute-start.49 = (f32[40,768]{1,0:T(8,128)S(1)}, f32[40,768]{1,0:T(8,128)S(1)}, u32[]{:S(2)}, u32[]{:S(2)}) collective-permute-start(f32[40,768]{1,0:T(8,128)S(1)} %add.28), channel_id=1, source_target_pairs={{0,8},{4,12},{8,0},{12,4},{16,24},{20,28},{24,16},{28,20},{1,9},{5... | collective-permute-start | bytes 368648 | tf_op jit(solution)/shard_map/ppermute | solution.py:999
  339.2 2.9 collective-permute-done.49
  342.0 3.7 %collective-permute-start.50 = (f32[40,768]{1,0:T(8,128)S(1)}, f32[40,768]{1,0:T(8,128)S(1)}, u32[]{:S(2)}, u32[]{:S(2)}) collective-permute-start(f32[40,768]{1,0:T(8,128)S(1)} %add.29), channel_id=1, source_target_pairs={{0,16},{4,20},{8,24},{12,28},{16,0},{20,4},{24,8},{28,12},{1,17},{... | collective-permute-start | bytes 368648 | tf_op jit(solution)/shard_map/ppermute | solution.py:999
  347.5 2.6 collective-permute-done.50
  350.7 6.2 %finish.1 = (f32[3,768]{1,0:T(4,128)}, f32[3072]{0:T(1024)}, f32[768]{0:T(1024)}, f32[768]{0:T(1024)}, f32[3,96,768]{2,1,0:T(8,128)}, /*index=5*/f32[96,3072]{1,...) custom-call(s32[4]{0:T(128)} %pad_add_fusion.place, ...), custom_call_target="tpu_custom_call" | custom-call | flops 1000000 | bytes 100000 | tf_op jit(solution)/shard_map/finish/pallas_call | solution.py:1015
  (213 shorter events, 65.1 us)
Async XLA Ops:
  5.1 14.9 %collective-permute-start.4 = (bf16[1,48,768]{2,1,0:T(8,128)(2,1)}, bf16[1,48,768]{2,1,0:T(8,128)(2,1)S(1)}, u32[]{:S(2)}, u32[]{:S(2)}) collective-permute-start(bf16[1,48,768]{2,1,0:T(8,128)(2,1)} %get-tuple-element.178), channel_id=1, source_target_pairs={{0,16},{4,20},{8,24},{12,28},{16,0},{20,4},{24,8},{28,12},{1,17},{... | collective-permute-start | bytes 221192 | tf_op jit(solution)/shard_map/ppermute | solution.py:968
  9.1 11.9 %collective-permute-start.5 = (bf16[1,48,768]{2,1,0:T(8,128)(2,1)}, bf16[1,48,768]{2,1,0:T(8,128)(2,1)S(1)}, u32[]{:S(2)}, u32[]{:S(2)}) collective-permute-start(bf16[1,48,768]{2,1,0:T(8,128)(2,1)} %get-tuple-element.178), channel_id=1, source_target_pairs={{0,24},{4,28},{8,0},{12,4},{16,8},{20,12},{24,16},{28,20},{1,25},{... | collective-permute-start | bytes 221192 | tf_op jit(solution)/shard_map/ppermute | solution.py:968
  10.5 10.6 %collective-permute-start.3 = (bf16[1,48,768]{2,1,0:T(8,128)(2,1)}, bf16[1,48,768]{2,1,0:T(8,128)(2,1)S(1)}, u32[]{:S(2)}, u32[]{:S(2)}) collective-permute-start(bf16[1,48,768]{2,1,0:T(8,128)(2,1)} %get-tuple-element.178), channel_id=1, source_target_pairs={{0,8},{4,12},{8,16},{12,20},{16,24},{20,28},{24,0},{28,4},{1,9},{5... | collective-permute-start | bytes 221192 | tf_op jit(solution)/shard_map/ppermute | solution.py:968
  11.1 10.0 %collective-permute-start = (bf16[2,48,768]{2,1,0:T(8,128)(2,1)}, bf16[2,48,768]{2,1,0:T(8,128)(2,1)S(1)}, u32[]{:S(2)}, u32[]{:S(2)}) collective-permute-start(bf16[2,48,768]{2,1,0:T(8,128)(2,1)} %get-tuple-element.177), channel_id=1, source_target_pairs={{0,8},{4,12},{8,16},{12,20},{16,24},{20,28},{24,0},{28,4},{1,9},{5... | collective-permute-start | bytes 442376 | tf_op jit(solution)/shard_map/ppermute | solution.py:968
  12.7 13.6 %collective-permute-start.1 = (bf16[2,48,768]{2,1,0:T(8,128)(2,1)}, bf16[2,48,768]{2,1,0:T(8,128)(2,1)S(1)}, u32[]{:S(2)}, u32[]{:S(2)}) collective-permute-start(bf16[2,48,768]{2,1,0:T(8,128)(2,1)} %get-tuple-element.177), channel_id=1, source_target_pairs={{0,16},{4,20},{8,24},{12,28},{16,0},{20,4},{24,8},{28,12},{1,17},{... | collective-permute-start | bytes 442376 | tf_op jit(solution)/shard_map/ppermute | solution.py:968
  27.5 24.7 %collective-permute-start.6 = (bf16[4,2,48,768]{3,2,1,0:T(8,128)(2,1)S(1)}, bf16[4,2,48,768]{3,2,1,0:T(8,128)(2,1)S(1)}, u32[]{:S(2)}, u32[]{:S(2)}) collective-permute-start(bf16[4,2,48,768]{3,2,1,0:T(8,128)(2,1)S(1)} %pad_maximum_fusion.2.refs_0_), channel_id=1, source_target_pairs={{0,4},{4,0},{8,12},{12,8},{16,20},{20,16},{24,28},{28,24},{1,5},{5... | collective-permute-start | bytes 1769480 | tf_op jit(solution)/shard_map/ppermute | solution.py:972
  29.3 12.3 %collective-permute-start.8 = (bf16[528,256]{1,0:T(8,128)(2,1)S(1)}, bf16[528,256]{1,0:T(8,128)(2,1)S(1)}, u32[]{:S(2)}, u32[]{:S(2)}) collective-permute-start(bf16[528,256]{1,0:T(8,128)(2,1)S(1)} %copy-done.32), channel_id=1, source_target_pairs={{0,8},{4,12},{8,16},{12,20},{16,24},{20,28},{24,0},{28,4},{1,9},{5... | collective-permute-start | bytes 811016 | tf_op jit(solution)/shard_map/ppermute | solution.py:968
  31.5 20.6 %collective-permute-start.9 = (bf16[528,256]{1,0:T(8,128)(2,1)S(1)}, bf16[528,256]{1,0:T(8,128)(2,1)S(1)}, u32[]{:S(2)}, u32[]{:S(2)}) collective-permute-start(bf16[528,256]{1,0:T(8,128)(2,1)S(1)} %copy-done.32), channel_id=1, source_target_pairs={{0,16},{4,20},{8,24},{12,28},{16,0},{20,4},{24,8},{28,12},{1,17},{... | collective-permute-start | bytes 811016 | tf_op jit(solution)/shard_map/ppermute | solution.py:968
  34.7 17.4 %collective-permute-start.10 = (bf16[528,256]{1,0:T(8,128)(2,1)S(1)}, bf16[528,256]{1,0:T(8,128)(2,1)S(1)}, u32[]{:S(2)}, u32[]{:S(2)}) collective-permute-start(bf16[528,256]{1,0:T(8,128)(2,1)S(1)} %copy-done.32), channel_id=1, source_target_pairs={{0,24},{4,28},{8,0},{12,4},{16,8},{20,12},{24,16},{28,20},{1,25},{... | collective-permute-start | bytes 811016 | tf_op jit(solution)/shard_map/ppermute | solution.py:968
  34.7 17.5 %collective-permute-start.7 = (bf16[4,1,48,768]{3,2,1,0:T(8,128)(2,1)S(1)}, bf16[4,1,48,768]{3,2,1,0:T(8,128)(2,1)S(1)}, u32[]{:S(2)}, u32[]{:S(2)}) collective-permute-start(bf16[4,1,48,768]{3,2,1,0:T(8,128)(2,1)S(1)} %pad_maximum_fusion.4.refs_4_), channel_id=1, source_target_pairs={{0,4},{4,0},{8,12},{12,8},{16,20},{20,16},{24,28},{28,24},{1,5},{5... | collective-permute-start | bytes 884744 | tf_op jit(solution)/shard_map/ppermute | solution.py:972
  57.0 44.0 %collective-permute-start.16 = (bf16[4,528,256]{2,1,0:T(8,128)(2,1)S(1)}, bf16[4,528,256]{2,1,0:T(8,128)(2,1)}, u32[]{:S(2)}, u32[]{:S(2)}) collective-permute-start(bf16[4,528,256]{2,1,0:T(8,128)(2,1)S(1)} %pad_maximum_fusion.1.refs_0_), channel_id=1, source_target_pairs={{0,4},{4,0},{8,12},{12,8},{16,20},{20,16},{24,28},{28,24},{1,5},{5... | collective-permute-start | bytes 3244040 | tf_op jit(solution)/shard_map/ppermute | solution.py:972
  57.5 43.4 %collective-permute-start.17 = (bf16[768,256]{1,0:T(8,128)(2,1)}, bf16[768,256]{1,0:T(8,128)(2,1)}, u32[]{:S(2)}, u32[]{:S(2)}) collective-permute-start(bf16[768,256]{1,0:T(8,128)(2,1)} %get-tuple-element.203), channel_id=1, source_target_pairs={{0,8},{4,12},{8,16},{12,20},{16,24},{20,28},{24,0},{28,4},{1,9},{5... | collective-permute-start | bytes 1179656 | tf_op jit(solution)/shard_map/ppermute | solution.py:968
  63.8 37.2 %collective-permute-start.18 = (bf16[768,256]{1,0:T(8,128)(2,1)}, bf16[768,256]{1,0:T(8,128)(2,1)}, u32[]{:S(2)}, u32[]{:S(2)}) collective-permute-start(bf16[768,256]{1,0:T(8,128)(2,1)} %get-tuple-element.203), channel_id=1, source_target_pairs={{0,16},{4,20},{8,24},{12,28},{16,0},{20,4},{24,8},{28,12},{1,17},{... | collective-permute-start | bytes 1179656 | tf_op jit(solution)/shard_map/ppermute | solution.py:968
  63.8 37.2 %collective-permute-start.19 = (bf16[768,256]{1,0:T(8,128)(2,1)}, bf16[768,256]{1,0:T(8,128)(2,1)}, u32[]{:S(2)}, u32[]{:S(2)}) collective-permute-start(bf16[768,256]{1,0:T(8,128)(2,1)} %get-tuple-element.203), channel_id=1, source_target_pairs={{0,24},{4,28},{8,0},{12,4},{16,8},{20,12},{24,16},{28,20},{1,25},{... | collective-permute-start | bytes 1179656 | tf_op jit(solution)/shard_map/ppermute | solution.py:968
  67.6 37.5 %collective-permute-start.15 = (bf16[4,528,256]{2,1,0:T(8,128)(2,1)S(1)}, bf16[4,528,256]{2,1,0:T(8,128)(2,1)}, u32[]{:S(2)}, u32[]{:S(2)}) collective-permute-start(bf16[4,528,256]{2,1,0:T(8,128)(2,1)S(1)} %pad_maximum_fusion.1.refs_0_), channel_id=1, source_target_pairs={{0,1},{1,0},{2,3},{3,2},{4,5},{5,4},{6,7},{7,6},{8,9},{9,8},{10,11... | collective-permute-start | bytes 3244040 | tf_op jit(solution)/shard_map/ppermute | solution.py:984
  107.0 36.8 %collective-permute-start.21 = (bf16[4,768,256]{2,1,0:T(8,128)(2,1)S(1)}, bf16[4,768,256]{2,1,0:T(8,128)(2,1)}, u32[]{:S(2)}, u32[]{:S(2)}) collective-permute-start(bf16[4,768,256]{2,1,0:T(8,128)(2,1)S(1)} %pad_maximum_fusion.refs_0_), channel_id=1, source_target_pairs={{0,4},{4,0},{8,12},{12,8},{16,20},{20,16},{24,28},{28,24},{1,5},{5... | collective-permute-start | bytes 4718600 | tf_op jit(solution)/shard_map/ppermute | solution.py:972
  107.0 36.8 %collective-permute-start.22 = (bf16[4,768,256]{2,1,0:T(8,128)(2,1)S(1)}, bf16[4,768,256]{2,1,0:T(8,128)(2,1)S(1)}, u32[]{:S(2)}, u32[]{:S(2)}) collective-permute-start(bf16[4,768,256]{2,1,0:T(8,128)(2,1)S(1)} %pad_maximum_fusion.refs_0_), channel_id=1, source_target_pairs={{0,1},{1,0},{2,3},{3,2},{4,5},{5,4},{6,7},{7,6},{8,9},{9,8},{10,11... | collective-permute-start | bytes 4718600 | tf_op jit(solution)/shard_map/ppermute | solution.py:984
  145.0 51.7 %collective-permute-start.24 = (bf16[8,384,256]{2,1,0:T(8,128)(2,1)}, bf16[8,384,256]{2,1,0:T(8,128)(2,1)S(1)}, u32[]{:S(2)}, u32[]{:S(2)}) collective-permute-start(bf16[8,384,256]{2,1,0:T(8,128)(2,1)} %get-tuple-element.226), channel_id=1, source_target_pairs={{0,1},{1,0},{2,3},{3,2},{4,5},{5,4},{6,7},{7,6},{8,9},{9,8},{10,11... | collective-permute-start | bytes 4718600 | tf_op jit(solution)/shard_map/ppermute | solution.py:984
  207.2 48.6 %collective-permute-start.27 = (bf16[4,768,256]{2,1,0:T(8,128)(2,1)}, bf16[4,768,256]{2,1,0:T(8,128)(2,1)S(1)}, u32[]{:S(2)}, u32[]{:S(2)}) collective-permute-start(bf16[4,768,256]{2,1,0:T(8,128)(2,1)} %get-tuple-element.252), channel_id=1, source_target_pairs={{0,4},{4,0},{8,12},{12,8},{16,20},{20,16},{24,28},{28,24},{1,5},{5... | collective-permute-start | bytes 4718600 | tf_op jit(solution)/shard_map/ppermute | solution.py:972
  207.4 48.3 %collective-permute-start.28 = (bf16[2,528,256]{2,1,0:T(8,128)(2,1)S(1)}, bf16[2,528,256]{2,1,0:T(8,128)(2,1)S(1)}, u32[]{:S(2)}, u32[]{:S(2)}) collective-permute-start(bf16[2,528,256]{2,1,0:T(8,128)(2,1)S(1)} %get-tuple-element.253), channel_id=1, source_target_pairs={{0,8},{4,12},{8,16},{12,20},{16,24},{20,28},{24,0},{28,4},{1,9},{5... | collective-permute-start | bytes 1622024 | tf_op jit(solution)/shard_map/ppermute | solution.py:968
  207.4 48.3 %collective-permute-start.29 = (bf16[2,528,256]{2,1,0:T(8,128)(2,1)S(1)}, bf16[2,528,256]{2,1,0:T(8,128)(2,1)S(1)}, u32[]{:S(2)}, u32[]{:S(2)}) collective-permute-start(bf16[2,528,256]{2,1,0:T(8,128)(2,1)S(1)} %get-tuple-element.254), channel_id=1, source_target_pairs={{0,16},{4,20},{8,24},{12,28},{16,0},{20,4},{24,8},{28,12},{1,17},{... | collective-permute-start | bytes 1622024 | tf_op jit(solution)/shard_map/ppermute | solution.py:968
  211.2 44.6 %collective-permute-start.30 = (bf16[2,528,256]{2,1,0:T(8,128)(2,1)S(1)}, bf16[2,528,256]{2,1,0:T(8,128)(2,1)S(1)}, u32[]{:S(2)}, u32[]{:S(2)}) collective-permute-start(bf16[2,528,256]{2,1,0:T(8,128)(2,1)S(1)} %get-tuple-element.255), channel_id=1, source_target_pairs={{0,24},{4,28},{8,0},{12,4},{16,8},{20,12},{24,16},{28,20},{1,25},{... | collective-permute-start | bytes 1622024 | tf_op jit(solution)/shard_map/ppermute | solution.py:968
  263.1 22.0 %collective-permute-start.32 = (bf16[8,432,128]{2,1,0:T(8,128)(2,1)S(1)}, bf16[8,432,128]{2,1,0:T(8,128)(2,1)S(1)}, u32[]{:S(2)}, u32[]{:S(2)}) collective-permute-start(bf16[8,432,128]{2,1,0:T(8,128)(2,1)S(1)} %get-tuple-element.267), channel_id=1, source_target_pairs={{0,2},{1,3},{2,0},{3,1},{4,6},{5,7},{6,4},{7,5},{8,10},{9,11},{10,... | collective-permute-start | bytes 2654216 | tf_op jit(solution)/shard_map/ppermute | solution.py:980
  264.7 21.6 %collective-permute-start.34 = (bf16[768,256]{1,0:T(8,128)(2,1)}, bf16[768,256]{1,0:T(8,128)(2,1)}, u32[]{:S(2)}, u32[]{:S(2)}) collective-permute-start(bf16[768,256]{1,0:T(8,128)(2,1)} %get-tuple-element.283), channel_id=1, source_target_pairs={{0,16},{4,20},{8,24},{12,28},{16,0},{20,4},{24,8},{28,12},{1,17},{... | collective-permute-start | bytes 1179656 | tf_op jit(solution)/shard_map/ppermute | solution.py:968
  266.5 19.9 %collective-permute-start.35 = (bf16[768,256]{1,0:T(8,128)(2,1)}, bf16[768,256]{1,0:T(8,128)(2,1)}, u32[]{:S(2)}, u32[]{:S(2)}) collective-permute-start(bf16[768,256]{1,0:T(8,128)(2,1)} %get-tuple-element.284), channel_id=1, source_target_pairs={{0,24},{4,28},{8,0},{12,4},{16,8},{20,12},{24,16},{28,20},{1,25},{... | collective-permute-start | bytes 1179656 | tf_op jit(solution)/shard_map/ppermute | solution.py:968
  270.1 26.2 %collective-permute-start.33 = (bf16[768,256]{1,0:T(8,128)(2,1)S(1)}, bf16[768,256]{1,0:T(8,128)(2,1)}, u32[]{:S(2)}, u32[]{:S(2)}) collective-permute-start(bf16[768,256]{1,0:T(8,128)(2,1)S(1)} %get-tuple-element.282), channel_id=1, source_target_pairs={{0,8},{4,12},{8,16},{12,20},{16,24},{20,28},{24,0},{28,4},{1,9},{5... | collective-permute-start | bytes 1179656 | tf_op jit(solution)/shard_map/ppermute | solution.py:968
  272.2 14.2 %collective-permute-start.36 = (bf16[528,256]{1,0:T(8,128)(2,1)}, bf16[528,256]{1,0:T(8,128)(2,1)}, u32[]{:S(2)}, u32[]{:S(2)}) collective-permute-start(bf16[528,256]{1,0:T(8,128)(2,1)} %get-tuple-element.290), channel_id=1, source_target_pairs={{0,4},{4,0},{8,12},{12,8},{16,20},{20,16},{24,28},{28,24},{1,5},{5... | collective-permute-start | bytes 811016 | tf_op jit(solution)/shard_map/ppermute | solution.py:972
  285.9 11.9 %collective-permute-start.37 = (bf16[4,432,128]{2,1,0:T(8,128)(2,1)S(1)}, bf16[4,432,128]{2,1,0:T(8,128)(2,1)S(1)}, u32[]{:S(2)}, u32[]{:S(2)}) collective-permute-start(bf16[4,432,128]{2,1,0:T(8,128)(2,1)S(1)} %get-tuple-element.291), channel_id=1, source_target_pairs={{0,4},{4,0},{8,12},{12,8},{16,20},{20,16},{24,28},{28,24},{1,5},{5... | collective-permute-start | bytes 1327112 | tf_op jit(solution)/shard_map/ppermute | solution.py:972
  298.6 16.0 %collective-permute-start.38 = (bf16[1296,256]{1,0:T(8,128)(2,1)S(1)}, bf16[1296,256]{1,0:T(8,128)(2,1)S(1)}, u32[]{:S(2)}, u32[]{:S(2)}) collective-permute-start(bf16[1296,256]{1,0:T(8,128)(2,1)S(1)} %z_sum.2), channel_id=1, source_target_pairs={{0,2},{1,3},{2,0},{3,1},{4,6},{5,7},{6,4},{7,5},{8,10},{9,11},{10,... | collective-permute-start | bytes 1990664 | tf_op jit(solution)/shard_map/ppermute | solution.py:980
  300.0 9.8 %collective-permute-start.39 = (bf16[432,128]{1,0:T(8,128)(2,1)S(1)}, bf16[432,128]{1,0:T(8,128)(2,1)S(1)}, u32[]{:S(2)}, u32[]{:S(2)}) collective-permute-start(bf16[432,128]{1,0:T(8,128)(2,1)S(1)} %get-tuple-element.301), channel_id=1, source_target_pairs={{0,8},{4,12},{8,16},{12,20},{16,24},{20,28},{24,0},{28,4},{1,9},{5... | collective-permute-start | bytes 331784 | tf_op jit(solution)/shard_map/ppermute | solution.py:968
  314.8 8.9 %collective-permute-start.42 = (f32[432,128]{1,0:T(8,128)S(1)}, f32[432,128]{1,0:T(8,128)S(1)}, u32[]{:S(2)}, u32[]{:S(2)}) collective-permute-start(f32[432,128]{1,0:T(8,128)S(1)} %z_sum.3.own), channel_id=1, source_target_pairs={{0,2},{1,3},{2,0},{3,1},{4,6},{5,7},{6,4},{7,5},{8,10},{9,11},{10,... | collective-permute-start | bytes 663560 | tf_op jit(solution)/shard_map/ppermute | solution.py:980
  332.3 9.7 %collective-permute-start.49 = (f32[40,768]{1,0:T(8,128)S(1)}, f32[40,768]{1,0:T(8,128)S(1)}, u32[]{:S(2)}, u32[]{:S(2)}) collective-permute-start(f32[40,768]{1,0:T(8,128)S(1)} %add.28), channel_id=1, source_target_pairs={{0,8},{4,12},{8,0},{12,4},{16,24},{20,28},{24,16},{28,20},{1,9},{5... | collective-permute-start | bytes 368648 | tf_op jit(solution)/shard_map/ppermute | solution.py:999
  (61 other events, 695.7 us)
